TPU v7x, 512 devices: a whole 4x4x16 slice. The times are simulated.
512 devices in a mesh: chan: 64 (over y_hi, z, core), tm: 8 (over y_lo, x).
Axes of the slice: x: 4, y: 4 (y_hi: 2, y_lo: 2; y = y_hi * 2 + y_lo), z: 16, core: 2. Of those that a mesh axis runs over, the one named last changes fastest.
Arguments:
- voltages: bfloat16 [1024, 96, 8192], P('chan', 'tm'), may hold values from -0.9921875 to 0.9921875, as said below
- eq_gain: float32 [1024, 4096], P('chan'), may hold values from 0.5 to 2
Outputs:
- visibilities: float32 [2, 4096, 32, 1024], P(None, ('chan', 'tm'))
Inputs may be any that keep to these rules, and one draw needn't show every extreme that they name: `voltages`: each sample is an integer of -127..127 divided by 128.
All inputs are finite; a program needn't handle non-finite values.
Results may differ from a plain program's by a relative error of at most 0.0078.
Values may be sent and summed in bfloat16 or wider, within the bound.
No kernel may reach another device: no remote copies, remote signals or barrier semaphores. Data moves between devices by JAX's collectives and lax.ppermute only.
A program may use at most 128 MiB of HBM per device.

v0:
```python
import math

import jax
import jax.numpy as jnp
import numpy as np
from jax import lax
from jax.sharding import PartitionSpec as P

FFT_LEN = 8192
TAPS = 16
LA = 128
REF = 32


def passed_along(value, axis, steps):
    count = lax.axis_size(axis)
    leading, last = (max(0, -steps), min(count, count - steps))
    return lax.ppermute(value, axis, [(source, source + steps) for source in range(leading, last)])


def make_tables(length, inner, taps_count):
    outer_len = length // inner
    outer_row = np.arange(outer_len)
    angle_one = 2.0 * np.pi * np.outer(outer_row, outer_row) / outer_len
    first_table = jnp.asarray(
        np.concatenate([np.cos(angle_one), -np.sin(angle_one)], axis=1), jnp.float32
    ).astype(jnp.bfloat16)
    inner_row = np.arange(inner)
    angle_twist = 2.0 * np.pi * np.outer(outer_row, inner_row) / length
    twist_cos = jnp.asarray(np.cos(angle_twist), jnp.float32)
    twist_sin = jnp.asarray(np.sin(angle_twist), jnp.float32)
    half_row = np.arange(inner // 2)
    angle_two = 2.0 * np.pi * np.outer(inner_row, half_row) / inner
    upper_rows = np.concatenate([np.cos(angle_two), -np.sin(angle_two)], axis=1)
    lower_rows = np.concatenate([np.sin(angle_two), np.cos(angle_two)], axis=1)
    second_table = jnp.asarray(
        np.concatenate([upper_rows, lower_rows], axis=0), jnp.float32
    ).astype(jnp.bfloat16)
    sample_pos = np.arange(taps_count * length)
    sinc_arg = np.pi * (sample_pos - taps_count * length / 2 + 0.5) / length
    proto = np.sin(sinc_arg) / sinc_arg
    proto = proto * (0.5 - 0.5 * np.cos(2.0 * np.pi * (sample_pos + 0.5) / (taps_count * length)))
    proto = proto / np.sqrt(np.mean(proto**2) * taps_count)
    tap_table = jnp.asarray(proto.reshape(taps_count, length)[::-1].copy(), jnp.float32)
    return (first_table, twist_cos, twist_sin, second_table, tap_table)


def spectra_block(framed_block, gains, tables, count):
    first_table, twist_cos, twist_sin, second_table, tap_table = tables
    taps_count = tap_table.shape[0]
    group_size = framed_block.shape[0]
    samples = framed_block.astype(jnp.float32)
    length = samples.shape[-1]
    filtered = tap_table[0] * samples[:, taps_count - 1 : taps_count - 1 + count]
    for lag in range(1, taps_count):
        filtered = (
            filtered
            + tap_table[lag] * samples[:, taps_count - 1 - lag : taps_count - 1 - lag + count]
        )
    filtered = filtered.astype(jnp.bfloat16)
    outer_len = first_table.shape[0]
    inner = twist_cos.shape[1]
    shaped = filtered.reshape(group_size, count, outer_len, inner)
    section_one = jnp.einsum(
        "gsba,bc->gsca", shaped, first_table, preferred_element_type=jnp.float32
    )
    real_one = section_one[:, :, :outer_len]
    imag_one = section_one[:, :, outer_len:]
    turned_real = real_one * twist_cos + imag_one * twist_sin
    turned_imag = imag_one * twist_cos - real_one * twist_sin
    turned = jnp.concatenate([turned_real, turned_imag], axis=-1).astype(jnp.bfloat16)
    section_two = jnp.einsum(
        "gskj,jm->gsmk", turned, second_table, preferred_element_type=jnp.float32
    )
    half = inner // 2
    scaled_gain = gains * (1.0 / math.sqrt(length))
    real_part = (
        section_two[:, :, :half].reshape(group_size, count, -1) * scaled_gain[:, None, :]
    ).astype(jnp.bfloat16)
    imag_part = (
        section_two[:, :, half:].reshape(group_size, count, -1) * scaled_gain[:, None, :]
    ).astype(jnp.bfloat16)
    return (real_part, imag_part)


def correlate(real_part, imag_part, inverse_count):
    ref_real = real_part[:REF]
    ref_imag = imag_part[:REF]
    real_real = jnp.einsum("itc,rtc->cri", real_part, ref_real, preferred_element_type=jnp.float32)
    imag_imag = jnp.einsum("itc,rtc->cri", imag_part, ref_imag, preferred_element_type=jnp.float32)
    imag_real = jnp.einsum("itc,rtc->cri", imag_part, ref_real, preferred_element_type=jnp.float32)
    real_imag = jnp.einsum("itc,rtc->cri", real_part, ref_imag, preferred_element_type=jnp.float32)
    return ((real_real + imag_imag) * inverse_count, (imag_real - real_imag) * inverse_count)


def shards(voltages, eq_gain):
    inputs_dev, slice_len, frame_len = voltages.shape
    channels = eq_gain.shape[1]
    needed = TAPS - 1
    hops = (needed + slice_len - 1) // slice_len
    pieces = []
    for hop in range(hops):
        taken = min(slice_len, needed - hop * slice_len)
        moved = passed_along(voltages[:, slice_len - taken :, :], "tm", hop + 1)
        pieces.insert(0, moved)
    framed = jnp.concatenate(pieces + [voltages], axis=1)
    tables = make_tables(FFT_LEN, LA, TAPS)
    group_size = math.gcd(inputs_dev, 4)
    blocks = inputs_dev // group_size

    def engine(pair):
        return spectra_block(pair[0], pair[1], tables, slice_len)

    framed_blocks = framed.reshape(blocks, group_size, slice_len + TAPS - 1, frame_len)
    gain_blocks = eq_gain.reshape(blocks, group_size, channels)
    spec_real, spec_imag = lax.map(engine, (framed_blocks, gain_blocks))
    spec_real = spec_real.reshape(inputs_dev, slice_len, channels)
    spec_imag = spec_imag.reshape(inputs_dev, slice_len, channels)
    count_tm = lax.axis_size("tm")
    owned_real, owned_imag = (
        lax.all_to_all(spec_real, "chan", split_axis=2, concat_axis=0, tiled=True),
        lax.all_to_all(spec_imag, "chan", split_axis=2, concat_axis=0, tiled=True),
    )
    whole_real, whole_imag = (
        lax.all_to_all(owned_real, "tm", split_axis=2, concat_axis=1, tiled=True),
        lax.all_to_all(owned_imag, "tm", split_axis=2, concat_axis=1, tiled=True),
    )
    inverse_count = 1.0 / (slice_len * count_tm)
    vis_real, vis_imag = correlate(whole_real, whole_imag, inverse_count)
    return jnp.stack([vis_real, vis_imag])


def solution(mesh):
    in_specs = (P("chan", "tm", None), P("chan", None))
    out_specs = P(None, ("chan", "tm"), None, None)
    return jax.shard_map(shards, mesh=mesh, in_specs=in_specs, out_specs=out_specs, check_vma=False)
```

profile of v0, /device:TPU:103, one launch (start us, length us, event | category | flops | bytes accessed | tf_op | source)
XLA Modules:
  0.0 494.7 jit_solution(17029248639485219831)
XLA Ops:
  0.0 3.1 collective-permute-start.1
  5.2 4.0 collective-permute-start
  10.3 16.7 %collective-permute-done = bf16[16,3,8192]{2,0,1:T(8,128)(2,1)} collective-permute-done((bf16[16,3,8192]{2,0,1:T(8,128)(2,1)}, bf16[16,3,8192]{2,0,1:T(8,128)(2,1)}, u32[]{:S(2)}, u32[]{:S(2)}) %collective-permute-start) | collective-permute-done | bytes 786464 | tf_op jit(solution)/shard_map/ppermute | solution.py:18
  27.0 44.1 %collective-permute-done.1 = bf16[16,12,8192]{2,0,1:T(8,128)(2,1)S(1)} collective-permute-done((bf16[16,12,8192]{2,0,1:T(8,128)(2,1)}, bf16[16,12,8192]{2,0,1:T(8,128)(2,1)S(1)}, u32[]{:S(2)}, u32[]{:S(2)}) %collective-permute-start.1) | collective-permute-done | bytes 3145760 | tf_op jit(solution)/shard_map/ppermute | solution.py:18
  71.1 5.5 %pad_maximum_fusion = bf16[16,27,8192]{2,0,1:T(8,128)(2,1)} fusion(bf16[16,12,8192]{2,0,1:T(8,128)(2,1)} %param.9, bf16[16,12,8192]{2,0,1:T(8,128)(2,1)S(1)} %collective-permute-done.1, bf16[16,3,8192]{2,0,1:T(8,128)(2,1)} %collective-permute-done), kind=kLoop, calls=%fused_computation.52 | loop fusion | flops 7077888 | bytes 14155776 | tf_op jit(solution)/shard_map/concatenate | solution.py:106
  76.6 12.6 %reshape.76 = bf16[4,4,27,8192]{3,1,0,2:T(4,128)(2,1)} reshape(bf16[16,27,8192]{2,0,1:T(8,128)(2,1)} %pad_maximum_fusion) | data formatting | bytes 14155776 | tf_op jit(solution)/shard_map/reshape | solution.py:114
  89.2 78.1 %while.14 = (s32[]{:T(128)}, bf16[4,4,12,4096]{3,1,0,2:T(4,128)(2,1)}, bf16[4,4,12,4096]{3,1,0,2:T(4,128)(2,1)}, bf16[4,4,27,8192]{3,1,0,2:T(4,128)(2,1)}, f32[4...) while((s32[]{:T(128)}, ...), condition=%wide.region_1.2_spmd.clone.clone, body=%wide.region_0.1_spmd.sunk.clone.clone.sunk | while | flops 322551808 | bytes 60703068 | solution.py:116
  91.1 7.0 %fusion.78 = bf16[4,12,8192]{2,0,1:T(4,128)(2,1)S(1)} fusion(f32[4,27,8192]{2,0,1:T(4,128)S(1)} %bitcast_convert_fusion.2, f32[8192]{0:T(1024)} %get-tuple-element.230, f32[8192]{0:T(1024)} %get-tuple-element.231, f32[8192]{0:T(1024)} %get-tuple-element.232, f32[8192]{0:T(1024)} %get-tuple-element.233, f32[8192]{0:T(1024)} %get-tuple-element.234, ...), kind=kLoop, calls=%fused_computation.6.clone.1 | loop fusion | flops 12582912 | bytes 26476544 | tf_op jit(solution)/shard_map/while/body/eval_jaxpr/convert_element_type | solution.py:60
  110.7 7.0 %fusion.78 = bf16[4,12,8192]{2,0,1:T(4,128)(2,1)S(1)} fusion(f32[4,27,8192]{2,0,1:T(4,128)S(1)} %bitcast_convert_fusion.2, f32[8192]{0:T(1024)} %get-tuple-element.230, f32[8192]{0:T(1024)} %get-tuple-element.231, f32[8192]{0:T(1024)} %get-tuple-element.232, f32[8192]{0:T(1024)} %get-tuple-element.233, f32[8192]{0:T(1024)} %get-tuple-element.234, ...), kind=kLoop, calls=%fused_computation.6.clone.1 | loop fusion | flops 12582912 | bytes 26476544 | tf_op jit(solution)/shard_map/while/body/eval_jaxpr/convert_element_type | solution.py:60
  130.2 7.0 %fusion.78 = bf16[4,12,8192]{2,0,1:T(4,128)(2,1)S(1)} fusion(f32[4,27,8192]{2,0,1:T(4,128)S(1)} %bitcast_convert_fusion.2, f32[8192]{0:T(1024)} %get-tuple-element.230, f32[8192]{0:T(1024)} %get-tuple-element.231, f32[8192]{0:T(1024)} %get-tuple-element.232, f32[8192]{0:T(1024)} %get-tuple-element.233, f32[8192]{0:T(1024)} %get-tuple-element.234, ...), kind=kLoop, calls=%fused_computation.6.clone.1 | loop fusion | flops 12582912 | bytes 26476544 | tf_op jit(solution)/shard_map/while/body/eval_jaxpr/convert_element_type | solution.py:60
  149.7 7.0 %fusion.78 = bf16[4,12,8192]{2,0,1:T(4,128)(2,1)S(1)} fusion(f32[4,27,8192]{2,0,1:T(4,128)S(1)} %bitcast_convert_fusion.2, f32[8192]{0:T(1024)} %get-tuple-element.230, f32[8192]{0:T(1024)} %get-tuple-element.231, f32[8192]{0:T(1024)} %get-tuple-element.232, f32[8192]{0:T(1024)} %get-tuple-element.233, f32[8192]{0:T(1024)} %get-tuple-element.234, ...), kind=kLoop, calls=%fused_computation.6.clone.1 | loop fusion | flops 12582912 | bytes 26476544 | tf_op jit(solution)/shard_map/while/body/eval_jaxpr/convert_element_type | solution.py:60
  167.3 2.4 reshape.78
  169.6 15.1 %copy.57 = bf16[16,12,4096]{0,1,2:T(8,128)(2,1)} copy(bf16[16,12,4096]{2,0,1:T(8,128)(2,1)S(1)} %reshape.78) | data formatting | bytes 3145728 | tf_op jit(solution)/shard_map/reshape | solution.py:117
  184.7 18.7 %reshape.93 = bf16[64,2,6144]{2,1,0:T(2,128)(2,1)} reshape(bf16[4096,12,16]{2,1,0:T(8,128)(2,1)} %bitcast.95) | data formatting | bytes 3145728
  203.4 19.8 %all-to-all-start = ((bf16[64,2,6144]{2,1,0:T(2,128)(2,1)}), bf16[64,2,6144]{2,1,0:T(2,128)(2,1)S(1)}, u32[]{:S(2)}, u32[]{:S(2)}) async-start(bf16[64,2,6144]{2,1,0:T(2,128)(2,1)} %reshape.93), calls=%async_computation | async-start | bytes 3145728 | tf_op jit(solution)/shard_map/all_to_all | solution.py:121
  223.3 2.4 reshape.79
  225.6 15.1 %copy.67 = bf16[16,12,4096]{0,1,2:T(8,128)(2,1)} copy(bf16[16,12,4096]{2,0,1:T(8,128)(2,1)S(1)} %reshape.79) | data formatting | bytes 3145728 | tf_op jit(solution)/shard_map/reshape | solution.py:118
  240.8 18.7 %reshape.95 = bf16[64,2,6144]{2,1,0:T(2,128)(2,1)} reshape(bf16[4096,12,16]{2,1,0:T(8,128)(2,1)} %bitcast.96) | data formatting | bytes 3145728
  259.5 41.1 %all-to-all-done = bf16[64,2,6144]{2,1,0:T(2,128)(2,1)S(1)} async-done(((bf16[64,2,6144]{2,1,0:T(2,128)(2,1)}), bf16[64,2,6144]{2,1,0:T(2,128)(2,1)S(1)}, u32[]{:S(2)}, u32[]{:S(2)}) %all-to-all-start) | async-done | bytes 1572896 | tf_op jit(solution)/shard_map/all_to_all | solution.py:121
  300.6 6.8 %all-to-all-start.2 = ((bf16[64,2,6144]{2,1,0:T(2,128)(2,1)}), bf16[64,2,6144]{2,1,0:T(2,128)(2,1)}, u32[]{:S(2)}, u32[]{:S(2)}) async-start(bf16[64,2,6144]{2,1,0:T(2,128)(2,1)} %reshape.95), calls=%async_computation.2 | async-start | bytes 3145728 | tf_op jit(solution)/shard_map/all_to_all | solution.py:122
  307.4 16.9 %reshape.94 = bf16[4096,12,16]{2,1,0:T(8,128)(2,1)} reshape(bf16[64,2,6144]{2,1,0:T(2,128)(2,1)S(1)} %all-to-all-done) | data formatting | bytes 3145728
  324.3 16.1 %copy.59 = bf16[64,16,12,64]{3,1,0,2:T(8,128)(2,1)S(1)} copy(bf16[64,16,12,64]{1,2,3,0:T(8,128)(2,1)} %bitcast.97) | data formatting | bytes 3145728 | tf_op jit(solution)/shard_map/all_to_all | solution.py:121
  340.4 3.9 copy.60
  344.3 40.3 %all-to-all-done.2 = bf16[64,2,6144]{2,1,0:T(2,128)(2,1)} async-done(((bf16[64,2,6144]{2,1,0:T(2,128)(2,1)}), bf16[64,2,6144]{2,1,0:T(2,128)(2,1)}, u32[]{:S(2)}, u32[]{:S(2)}) %all-to-all-start.2) | async-done | bytes 1572896 | tf_op jit(solution)/shard_map/all_to_all | solution.py:122
  384.7 20.1 %all-to-all-start.1 = ((bf16[1024,12,64]{0,1,2:T(8,128)(2,1)}), bf16[1024,12,64]{0,1,2:T(8,128)(2,1)S(1)}, u32[]{:S(2)}, u32[]{:S(2)}) async-start(bf16[1024,12,64]{0,1,2:T(8,128)(2,1)} %copy.60), calls=%async_computation.1 | async-start | bytes 4194304 | tf_op jit(solution)/shard_map/all_to_all | solution.py:125
  404.8 18.0 %reshape.96 = bf16[4096,12,16]{2,1,0:T(8,128)(2,1)} reshape(bf16[64,2,6144]{2,1,0:T(2,128)(2,1)} %all-to-all-done.2) | data formatting | bytes 3145728
  422.8 16.8 %copy.69 = bf16[64,16,12,64]{3,1,0,2:T(8,128)(2,1)} copy(bf16[64,16,12,64]{1,2,3,0:T(8,128)(2,1)} %bitcast.98) | data formatting | bytes 3145728 | tf_op jit(solution)/shard_map/all_to_all | solution.py:122
  439.6 5.5 %copy.70 = bf16[1024,12,64]{0,1,2:T(8,128)(2,1)} copy(bf16[1024,12,64]{2,0,1:T(8,128)(2,1)} %bitcast.105) | data formatting | bytes 3145728 | tf_op jit(solution)/shard_map/all_to_all | solution.py:122
  445.1 5.1 %all-to-all-start.3 = ((bf16[1024,12,64]{0,1,2:T(8,128)(2,1)}), bf16[1024,12,64]{0,1,2:T(8,128)(2,1)}, u32[]{:S(2)}, u32[]{:S(2)}) async-start(bf16[1024,12,64]{0,1,2:T(8,128)(2,1)} %copy.70), calls=%async_computation.3 | async-start | bytes 4194304 | tf_op jit(solution)/shard_map/all_to_all | solution.py:126
  453.5 27.1 %all-to-all-done.3 = bf16[1024,12,64]{0,1,2:T(8,128)(2,1)} async-done(((bf16[1024,12,64]{0,1,2:T(8,128)(2,1)}), bf16[1024,12,64]{0,1,2:T(8,128)(2,1)}, u32[]{:S(2)}, u32[]{:S(2)}) %all-to-all-start.3) | async-done | bytes 1572896 | tf_op jit(solution)/shard_map/all_to_all | solution.py:126
  480.5 2.5 copy.73
  483.1 2.5 copy.117
  (100 shorter events, 65.1 us)
Async XLA Ops:
  0.0 71.1 %collective-permute-start.1 = (bf16[16,12,8192]{2,0,1:T(8,128)(2,1)}, bf16[16,12,8192]{2,0,1:T(8,128)(2,1)S(1)}, u32[]{:S(2)}, u32[]{:S(2)}) collective-permute-start(bf16[16,12,8192]{2,0,1:T(8,128)(2,1)} %param.9), channel_id=1, source_target_pairs={{0,1},{1,2},{2,3},{3,4},{4,5},{5,6},{6,7},{8,9},{9,10},{10,11},{11... | collective-permute-start | bytes 9437192 | tf_op jit(solution)/shard_map/ppermute | solution.py:18
  5.2 21.8 %collective-permute-start = (bf16[16,3,8192]{2,0,1:T(8,128)(2,1)}, bf16[16,3,8192]{2,0,1:T(8,128)(2,1)}, u32[]{:S(2)}, u32[]{:S(2)}) collective-permute-start(bf16[16,3,8192]{2,0,1:T(8,128)(2,1)} %slice.123), channel_id=1, source_target_pairs={{0,2},{1,3},{2,4},{3,5},{4,6},{5,7},{8,10},{9,11},{10,12},{11,13},... | collective-permute-start | bytes 2359304 | tf_op jit(solution)/shard_map/ppermute | solution.py:18
  76.6 12.6 %copy-start.2 = (bf16[256,128,1,1]{1,0,3,2:T(8,128)(2,1)S(1)}, bf16[256,128,1,1]{1,0,3,2:T(8,128)(2,1)}, u32[]{:S(2)}) copy-start(bf16[256,128,1,1]{1,0,3,2:T(8,128)(2,1)} %constant.151) | copy-start | bytes 196612
  76.6 12.6 %copy-start.3 = (f32[64,128]{1,0:T(8,128)S(1)}, f32[64,128]{1,0:T(8,128)}, u32[]{:S(2)}) copy-start(f32[64,128]{1,0:T(8,128)} %constant.31.clone..sunk.3) | copy-start | bytes 98308
  76.6 12.6 %copy-start.5 = (f32[64,128]{1,0:T(8,128)S(1)}, f32[64,128]{1,0:T(8,128)}, u32[]{:S(2)}) copy-start(f32[64,128]{1,0:T(8,128)} %constant.32.clone..sunk.3) | copy-start | bytes 98308
  76.6 12.6 %copy-start.7 = (bf16[64,128,1,1]{1,0,3,2:T(8,128)(2,1)S(1)}, bf16[64,128,1,1]{1,0,3,2:T(8,128)(2,1)}, u32[]{:S(2)}) copy-start(bf16[64,128,1,1]{1,0,3,2:T(8,128)(2,1)} %constant.152) | copy-start | bytes 49156
  106.4 1.1 copy-start
  107.5 1.2 copy-start.4
  107.5 1.2 copy-start.6
  125.9 1.1 copy-start
  127.0 1.2 copy-start.4
  127.0 1.2 copy-start.6
  145.4 1.1 copy-start
  146.5 1.2 copy-start.4
  146.5 1.2 copy-start.6
  164.9 1.1 copy-start
  166.0 1.2 copy-start.4
  166.0 1.2 copy-start.6
  203.4 97.1 %all-to-all-start = ((bf16[64,2,6144]{2,1,0:T(2,128)(2,1)}), bf16[64,2,6144]{2,1,0:T(2,128)(2,1)S(1)}, u32[]{:S(2)}, u32[]{:S(2)}) async-start(bf16[64,2,6144]{2,1,0:T(2,128)(2,1)} %reshape.93), calls=%async_computation | async-start | bytes 3145728 | tf_op jit(solution)/shard_map/all_to_all | solution.py:121
  300.6 84.1 %all-to-all-start.2 = ((bf16[64,2,6144]{2,1,0:T(2,128)(2,1)}), bf16[64,2,6144]{2,1,0:T(2,128)(2,1)}, u32[]{:S(2)}, u32[]{:S(2)}) async-start(bf16[64,2,6144]{2,1,0:T(2,128)(2,1)} %reshape.95), calls=%async_computation.2 | async-start | bytes 3145728 | tf_op jit(solution)/shard_map/all_to_all | solution.py:122
  384.7 60.4 %all-to-all-start.1 = ((bf16[1024,12,64]{0,1,2:T(8,128)(2,1)}), bf16[1024,12,64]{0,1,2:T(8,128)(2,1)S(1)}, u32[]{:S(2)}, u32[]{:S(2)}) async-start(bf16[1024,12,64]{0,1,2:T(8,128)(2,1)} %copy.60), calls=%async_computation.1 | async-start | bytes 4194304 | tf_op jit(solution)/shard_map/all_to_all | solution.py:125
  445.1 35.5 %all-to-all-start.3 = ((bf16[1024,12,64]{0,1,2:T(8,128)(2,1)}), bf16[1024,12,64]{0,1,2:T(8,128)(2,1)}, u32[]{:S(2)}, u32[]{:S(2)}) async-start(bf16[1024,12,64]{0,1,2:T(8,128)(2,1)} %copy.70), calls=%async_computation.3 | async-start | bytes 4194304 | tf_op jit(solution)/shard_map/all_to_all | solution.py:126
  487.7 1.8 copy-start.1
where the time goes:
time: 498 us; the launch traced here: 495 us
  local copies, waits for them, and re-layouts  204 us (41%)
  waiting for transfers between devices  169 us (34%)
  starting transfers between devices  59.1 us (12%)
  other arithmetic  49.5 us (10%)
  matrix products  12.1 us (2%)
    unnamed x14, local copies, waits for them, and re-layouts  72.3 us
    ppermute x2, waiting for transfers between devices, passed_along(): lax.ppermute(value, axis, [(source, source + steps) for source in range(l...  60.8 us
    all_to_all x1, waiting for transfers between devices, shards(): lax.all_to_all(spec_real, 'chan', split_axis=2, concat_axis=0, tiled=True)  41.1 us
    all_to_all x1, waiting for transfers between devices, shards(): lax.all_to_all(spec_imag, 'chan', split_axis=2, concat_axis=0, tiled=True)  40.3 us
    convert_element_type x4, other arithmetic, spectra_block(): filtered = filtered.astype(jnp.bfloat16)  28.2 us
    all_to_all x1, waiting for transfers between devices, shards(): lax.all_to_all(owned_imag, 'tm', split_axis=2, concat_axis=1, tiled=True)  27.1 us
    all_to_all x2, local copies, waits for them, and re-layouts, shards(): lax.all_to_all(spec_imag, 'chan', split_axis=2, concat_axis=0, tiled=True)  22.3 us
    all_to_all x1, starting transfers between devices, shards(): lax.all_to_all(owned_real, 'tm', split_axis=2, concat_axis=1, tiled=True)  20.1 us
  transfers between devices with their start and end apart: 6, of which 5 were waited for; matrix products, arithmetic and copies ran while one was open for 24% of the time, Pallas kernels for 0%

commit v1 on v0

v1 whole, which is shorter than its diff:
```python
import math

import jax
import jax.numpy as jnp
import numpy as np
from jax import lax
from jax.experimental import pallas as pl
from jax.experimental.pallas import tpu as pltpu
from jax.sharding import Mesh, PartitionSpec as P

FFT_LEN = 8192
TAPS = 16
LA = 128
REF = 32
OUTER = FFT_LEN // LA
SPECTRA = 96
STEP = 16
LEAD = 16
VMEM = 56 * 1024 * 1024


def make_tables():
    outer_row = np.arange(OUTER)
    angle_one = 2.0 * np.pi * np.outer(outer_row, outer_row) / OUTER
    first_table = np.concatenate([np.cos(angle_one), -np.sin(angle_one)], axis=1)
    inner_row = np.arange(LA)
    angle_twist = 2.0 * np.pi * np.outer(outer_row, inner_row) / FFT_LEN
    half_row = np.arange(LA // 2)
    angle_two = 2.0 * np.pi * np.outer(inner_row, half_row) / LA
    upper_rows = np.concatenate([np.cos(angle_two), -np.sin(angle_two)], axis=1)
    lower_rows = np.concatenate([np.sin(angle_two), np.cos(angle_two)], axis=1)
    second_table = np.concatenate([upper_rows, lower_rows], axis=0)
    second_table = second_table.reshape(2 * LA, 2, 32, 2).transpose(0, 3, 1, 2).reshape(2 * LA, LA)
    sample_pos = np.arange(TAPS * FFT_LEN)
    sinc_arg = np.pi * (sample_pos - TAPS * FFT_LEN / 2 + 0.5) / FFT_LEN
    proto = np.sin(sinc_arg) / sinc_arg
    proto = proto * (0.5 - 0.5 * np.cos(2.0 * np.pi * (sample_pos + 0.5) / (TAPS * FFT_LEN)))
    proto = proto / np.sqrt(np.mean(proto**2) * TAPS)
    taps = proto.reshape(TAPS, FFT_LEN)[::-1].reshape(TAPS, OUTER, LA)
    return (
        jnp.asarray(first_table.T, jnp.float32).astype(jnp.bfloat16),
        jnp.asarray(np.cos(angle_twist), jnp.float32),
        jnp.asarray(np.sin(angle_twist), jnp.float32),
        jnp.asarray(second_table, jnp.float32).astype(jnp.bfloat16),
        jnp.asarray(taps, jnp.float32),
    )


def frames_kernel(x_ref, o_ref, wide):
    for b in range(OUTER):
        wide[pl.ds(16 * b, 16), :] = x_ref[0, :, b * LA : (b + 1) * LA].astype(jnp.float32)
    for i in range(16):
        for h in range(4):
            rows = wide[pl.ds(256 * h + i, 16, stride=16), :]
            o_ref[i // 2, i % 2, 0, h * 16 : (h + 1) * 16, :] = rows.astype(jnp.bfloat16)


def to_frames(by_time):
    times, inputs, _ = by_time.shape
    return pl.pallas_call(
        frames_kernel,
        grid=(times,),
        in_specs=[pl.BlockSpec((1, inputs, FFT_LEN), lambda s: (s, 0, 0))],
        out_specs=pl.BlockSpec((8, 2, 1, OUTER, LA), lambda s: (0, 0, s, 0, 0)),
        out_shape=jax.ShapeDtypeStruct((8, 2, times, OUTER, LA), jnp.bfloat16),
        scratch_shapes=[pltpu.VMEM((inputs * OUTER, LA), jnp.float32)],
        compiler_params=pltpu.CompilerParams(vmem_limit_bytes=VMEM),
        name="frames",
    )(by_time)


def spectra_kernel(x_ref, gain_ref, first_ref, cos_ref, sin_ref, second_ref, taps_ref, o_ref, held, filt, spec):
    chunk = pl.program_id(0)

    @pl.when(chunk == 0)
    def _():
        for i in range(2):
            held[i, 0:LEAD] = jnp.zeros((LEAD, OUTER, LA), jnp.bfloat16)
            for t in range(8):
                held[i, LEAD + 12 * t : LEAD + 12 * t + 12] = x_ref[t, i]

    base = chunk * STEP

    def filter_step(n, carry):
        i = n // 4
        row = pl.multiple_of((n % 4) * 16, 16)
        for group in range(STEP // 8):
            acc = [None] * 8
            for m in range(8 + TAPS - 1):
                v = held[i, base + (LEAD - TAPS + 1) + group * 8 + m, pl.ds(row, 16), :].astype(jnp.float32)
                for j in range(8):
                    p = j + TAPS - 1 - m
                    if 0 <= p < TAPS:
                        term = taps_ref[p, pl.ds(row, 16), :] * v
                        acc[j] = term if acc[j] is None else acc[j] + term
            for j in range(8):
                filt[i * (STEP // 4) + group * 2 + j // 4, pl.ds(row, 16), (j % 4) * LA : (j % 4 + 1) * LA] = acc[
                    j
                ].astype(jnp.bfloat16)
        return carry

    lax.fori_loop(0, 8, filter_step, 0)

    first = first_ref[...]
    second = second_ref[...]

    def transform_step(g, carry):
        i = g // (STEP // 4)
        part = jnp.dot(first, filt[g], preferred_element_type=jnp.float32)
        cos = cos_ref[...]
        sin = sin_ref[...]
        rows = []
        for f in range(4):
            u = part[:OUTER, f * LA : (f + 1) * LA]
            v = part[OUTER:, f * LA : (f + 1) * LA]
            rows.append(jnp.concatenate([u * cos + v * sin, v * cos - u * sin], axis=1).astype(jnp.bfloat16))
        turned = jnp.concatenate(rows, axis=0)
        whole = jnp.dot(turned, second, preferred_element_type=jnp.float32)
        gain = gain_ref[i]
        for f in range(4):
            spec[i, pl.ds(((g % (STEP // 4)) * 4 + f) * OUTER, OUTER), :] = whole[f * OUTER : (f + 1) * OUTER] * gain
        return carry

    lax.fori_loop(0, 2 * (STEP // 4), transform_step, 0)

    low = lax.broadcasted_iota(jnp.int32, (STEP, LA), 1) < LA // 2
    for k in range(OUTER):
        y0 = spec[0, pl.ds(k, STEP, stride=OUTER), :]
        y1 = spec[1, pl.ds(k, STEP, stride=OUTER), :]
        o_ref[0, k // 8, k % 8] = jnp.where(low, y0, pltpu.roll(y1, LA // 2, 1)).astype(jnp.bfloat16)
        o_ref[1, k // 8, k % 8] = jnp.where(low, pltpu.roll(y0, LA // 2, 1), y1).astype(jnp.bfloat16)


def spectra(framed, gain, tables):
    whole = lambda *shape: pl.BlockSpec(shape, lambda s: (0,) * len(shape))
    return pl.pallas_call(
        spectra_kernel,
        grid=(SPECTRA // STEP,),
        in_specs=[
            whole(8, 2, 12, OUTER, LA),
            whole(2, OUTER, LA),
            whole(LA, OUTER),
            whole(OUTER, LA),
            whole(OUTER, LA),
            whole(2 * LA, LA),
            whole(TAPS, OUTER, LA),
        ],
        out_specs=pl.BlockSpec((2, 8, 8, STEP, LA), lambda s: (0, 0, 0, s, 0)),
        out_shape=jax.ShapeDtypeStruct((2, 8, 8, SPECTRA, LA), jnp.bfloat16),
        scratch_shapes=[
            pltpu.VMEM((2, LEAD + SPECTRA, OUTER, LA), jnp.bfloat16),
            pltpu.VMEM((2 * (STEP // 4), OUTER, 4 * LA), jnp.bfloat16),
            pltpu.VMEM((2, STEP * OUTER, LA), jnp.float32),
        ],
        compiler_params=pltpu.CompilerParams(vmem_limit_bytes=VMEM),
        name="spectra",
    )(framed, gain, *tables)


def cross_kernel(x_ref, r_ref, o_ref, tx, tr):
    pad = jnp.zeros((LA - SPECTRA, LA), jnp.float32)
    for half in range(2):
        for s in range(16):
            for src, dst in ((x_ref, tx), (r_ref, tr)):
                block = jnp.concatenate([src[s, half].astype(jnp.float32), pad], axis=0)
                dst[half, pl.ds(s * LA, LA), :] = block.T

    def channel(q, carry):
        parts = []
        for half in range(2):
            xr = tx[half, pl.ds(q, 32, stride=64), :].astype(jnp.bfloat16)
            xi = tx[half, pl.ds(q + 32, 32, stride=64), :].astype(jnp.bfloat16)
            rr = tr[half, pl.ds(q, 32, stride=64), :].astype(jnp.bfloat16)
            ri = tr[half, pl.ds(q + 32, 32, stride=64), :].astype(jnp.bfloat16)
            left = jnp.concatenate([xr, xi], axis=1)
            right = jnp.concatenate(
                [jnp.concatenate([rr, ri], axis=1), jnp.concatenate([-ri, rr], axis=1)], axis=0
            )
            parts.append(
                lax.dot_general(left, right, (((1,), (1,)), ((), ())), preferred_element_type=jnp.float32)
            )
        both = jnp.concatenate(parts, axis=1) * (1.0 / SPECTRA)
        o_ref[q, 0] = both.astype(jnp.bfloat16)
        return carry

    lax.fori_loop(0, 32, channel, 0)


def cross(own, refs):
    block = pl.BlockSpec((16, 2, SPECTRA, LA), lambda r: (0, r, 0, 0))
    return pl.pallas_call(
        cross_kernel,
        grid=(4,),
        in_specs=[block, block],
        out_specs=pl.BlockSpec((32, 1, 32, LA), lambda r: (0, r, 0, 0)),
        out_shape=jax.ShapeDtypeStruct((32, 4, 32, LA), jnp.bfloat16),
        scratch_shapes=[pltpu.VMEM((2, 16 * LA, LA), jnp.float32)] * 2,
        compiler_params=pltpu.CompilerParams(vmem_limit_bytes=VMEM),
        name="cross",
    )(own, refs)


def turn_kernel(x_ref, o_ref):
    for n in range(8):
        block = jnp.concatenate([x_ref[4 * n + m, 0] for m in range(4)], axis=0).astype(jnp.float32).T
        for r in range(2):
            for part in range(2):
                o_ref[part, r, :, n * LA : (n + 1) * LA] = block[r * 64 + part * 32 : r * 64 + part * 32 + 32]


def turn(pieces):
    return pl.pallas_call(
        turn_kernel,
        grid=(4,),
        in_specs=[pl.BlockSpec((32, 1, 32, LA), lambda r: (0, r, 0, 0))],
        out_specs=pl.BlockSpec((2, 2, REF, 1024), lambda r: (0, r, 0, 0)),
        out_shape=jax.ShapeDtypeStruct((2, 8, REF, 1024), jnp.float32),
        compiler_params=pltpu.CompilerParams(vmem_limit_bytes=VMEM),
        name="turn",
    )(pieces)


def shards(voltages, eq_gain):
    tables = make_tables()
    frames = to_frames(jnp.swapaxes(voltages, 0, 1))
    framed = lax.all_to_all(frames, ("yl", "x"), 0, 0, tiled=True)
    mine = lax.axis_index("yl") * 4 + lax.axis_index("x")
    gain = lax.dynamic_slice(eq_gain, (2 * mine, 0), (2, eq_gain.shape[1])) * (1.0 / math.sqrt(FFT_LEN))
    gain = gain.reshape(2, 32, 2, OUTER).transpose(0, 3, 2, 1)
    gain = jnp.stack([gain, gain], axis=3).reshape(2, OUTER, LA)
    spec = spectra(framed, gain, tables)
    own = lax.all_to_all(spec.reshape(16, 8, SPECTRA, LA), ("core", "yl", "x"), 0, 0, tiled=True)
    first = (lax.axis_index("yh") == 0) & (lax.axis_index("z") == 0)
    refs = lax.psum(jnp.where(first, own, jnp.zeros_like(own)), ("yh", "z"))
    pieces = cross(own, refs)
    pieces = lax.all_to_all(pieces, ("yh", "z"), 0, 0, tiled=True)
    return turn(pieces)


def solution(mesh):
    fine = Mesh(mesh.devices.reshape(2, 16, 2, 2, 4), ("yh", "z", "core", "yl", "x"))
    chan, tm = ("yh", "z", "core"), ("yl", "x")
    return jax.shard_map(
        shards,
        mesh=fine,
        in_specs=(P(chan, tm, None), P(chan, None)),
        out_specs=P(None, chan + tm, None, None),
        check_vma=False,
    )
```

time: 498 us -> 553 us (1.11)
  the two profiles are of different devices: /device:TPU:103 before, /device:TPU:34 now
where the time goes in v1:
time: 553 us
  waiting for transfers between devices  396 us (72%)
  Pallas kernels  81.7 us (15%)
  blocking collectives  42.6 us (8%)
  between operations  13.4 us (2%)
  starting transfers between devices  13.2 us (2%)
    psum x1, waiting for transfers between devices, shards(): refs = lax.psum(jnp.where(first, own, jnp.zeros_like(own)), ('yh', 'z'))  315 us
    all_to_all x1, blocking collectives, shards(): pieces = lax.all_to_all(pieces, ('yh', 'z'), 0, 0, tiled=True)  42.6 us
    all_to_all x1, waiting for transfers between devices, shards(): framed = lax.all_to_all(frames, ('yl', 'x'), 0, 0, tiled=True)  41 us
    all_to_all x1, waiting for transfers between devices, shards(): lax.all_to_all(spec.reshape(16, 8, SPECTRA, LA), ('core', 'yl', 'x'), 0,...  39.7 us
    pallas_call x1, Pallas kernels, cross(): pl.pallas_call(cross_kernel, grid=(4,), in_specs=[block, block], out_spec...  37.8 us
    pallas_call x1, Pallas kernels, spectra(): pl.pallas_call(spectra_kernel, grid=(SPECTRA // STEP,), in_specs=[whole(8...  31.3 us
  transfers between devices with their start and end apart: 3, of which 3 were waited for; matrix products, arithmetic and copies ran while one was open for 0% of the time, Pallas kernels for 0%

profile of v1, /device:TPU:34, one launch (start us, length us, event | category | flops | bytes accessed | tf_op | source)
XLA Modules:
  0.0 552.9 jit_solution(2455806634079138400)
XLA Ops:
  6.5 8.8 %frames.1 = bf16[8,2,12,64,128]{4,3,2,1,0:T(8,128)(2,1)} custom-call(bf16[12,16,8192]{2,1,0:T(8,128)(2,1)} %bitcast.9), custom_call_target="tpu_custom_call" | custom-call | tf_op jit(solution)/shard_map/frames/pallas_call | solution.py:60
  15.3 5.8 %all-to-all-start = ((bf16[8,2,12,64,128]{4,3,2,1,0:T(8,128)(2,1)}), bf16[8,2,12,64,128]{4,3,2,1,0:T(8,128)(2,1)S(1)}, u32[]{:S(2)}, u32[]{:S(2)}) async-start(bf16[8,2,12,64,128]{4,3,2,1,0:T(8,128)(2,1)} %frames.1), calls=%async_computation | async-start | bytes 6291456 | tf_op jit(solution)/shard_map/all_to_all | solution.py:226
  21.2 0.9 dynamic-slice_multiply_fusion
  22.1 0.1 reshape.9
  22.3 0.7 copy.10.gain_ref
  23.0 41.0 %all-to-all-done.x_ref = bf16[8,2,12,64,128]{4,3,2,1,0:T(8,128)(2,1)S(1)} async-done(((bf16[8,2,12,64,128]{4,3,2,1,0:T(8,128)(2,1)}), bf16[8,2,12,64,128]{4,3,2,1,0:T(8,128)(2,1)S(1)}, u32[]{:S(2)}, u32[]{:S(2)}) %all-to-all-start) | async-done | bytes 3145760 | tf_op jit(solution)/shard_map/all_to_all | solution.py:226
  64.0 0.0 copy-start.1
  64.0 1.6 copy-done.1
  65.7 31.3 %spectra.1 = bf16[2,8,8,96,128]{4,3,2,1,0:T(8,128)(2,1)} custom-call(bf16[8,2,12,64,128]{4,3,2,1,0:T(8,128)(2,1)} %copy-done.1, f32[2,64,128]{2,1,0:T(8,128)} %copy.10.gain_ref, bf16[128,64]{1,0:T(8,128)(2,1)} %constant.47.first_ref, f32[64,128]{1,0:T(8,128)} %constant.41.clone.cos_ref, f32[64,128]{1,0:T(8,128)} %constant.42.clone.sin_ref, ...), custom_call_target="tpu_custom_call" | custom-call | tf_op jit(solution)/shard_map/spectra/pallas_call | solution.py:136
  97.0 7.3 %all-to-all-start.1 = ((bf16[16,8,96,128]{3,2,1,0:T(8,128)(2,1)}), bf16[16,8,96,128]{3,2,1,0:T(8,128)(2,1)S(1)}, u32[]{:S(2)}, u32[]{:S(2)}) async-start(bf16[16,8,96,128]{3,2,1,0:T(8,128)(2,1)} %bitcast.8), calls=%async_computation.1 | async-start | bytes 6291456 | tf_op jit(solution)/shard_map/all_to_all | solution.py:232
  104.3 0.0 all-reduce.2.cloned.1.call-start
  104.3 39.7 %all-to-all-done.1.x_ref = bf16[16,8,96,128]{3,2,1,0:T(8,128)(2,1)S(1)} async-done(((bf16[16,8,96,128]{3,2,1,0:T(8,128)(2,1)}), bf16[16,8,96,128]{3,2,1,0:T(8,128)(2,1)S(1)}, u32[]{:S(2)}, u32[]{:S(2)}) %all-to-all-start.1) | async-done | bytes 3145760 | tf_op jit(solution)/shard_map/all_to_all | solution.py:232
  144.0 0.0 copy-start
  144.0 2.0 broadcast_select_fusion
  146.1 0.6 copy-done
  146.7 0.0 all-reduce.2.cloned.1.call-update
  146.7 315.1 %all-reduce.2.cloned.1.call-done.r_ref = bf16[16,8,96,128]{3,2,1,0:T(8,128)(2,1)} async-done(((bf16[16,8,96,128]{3,2,1,0:T(8,128)(2,1)}), bf16[16,8,96,128]{3,2,1,0:T(8,128)(2,1)}) %all-reduce.2.cloned.1.call-update) | async-done | bytes 3145744 | tf_op jit(solution)/shard_map/psum | solution.py:234
  461.9 37.8 %cross.1 = bf16[32,4,32,128]{3,2,1,0:T(8,128)(2,1)} custom-call(bf16[16,8,96,128]{3,2,1,0:T(8,128)(2,1)} %copy-done, bf16[16,8,96,128]{3,2,1,0:T(8,128)(2,1)} %all-reduce.2.cloned.1.call-done.r_ref), custom_call_target="tpu_custom_call" | custom-call | tf_op jit(solution)/shard_map/cross/pallas_call | solution.py:191
  499.6 42.6 %all_to_all.15.x_ref = bf16[32,4,32,128]{3,2,1,0:T(8,128)(2,1)} all-to-all(bf16[32,4,32,128]{3,2,1,0:T(8,128)(2,1)} %cross.1), channel_id=1, replica_groups=mesh['yh'=2,'z'=16,'core'=2,'yl'=2,'x'=4] {'yh','z'}, dimensions={0} | all-to-all | bytes 2097152 | tf_op jit(solution)/shard_map/all_to_all | solution.py:236
  542.2 3.8 turn.1
  (2 shorter events, 0.0 us)
Async XLA Ops:
  15.3 48.7 %all-to-all-start = ((bf16[8,2,12,64,128]{4,3,2,1,0:T(8,128)(2,1)}), bf16[8,2,12,64,128]{4,3,2,1,0:T(8,128)(2,1)S(1)}, u32[]{:S(2)}, u32[]{:S(2)}) async-start(bf16[8,2,12,64,128]{4,3,2,1,0:T(8,128)(2,1)} %frames.1), calls=%async_computation | async-start | bytes 6291456 | tf_op jit(solution)/shard_map/all_to_all | solution.py:226
  64.0 1.6 copy-start.1
  97.0 47.0 %all-to-all-start.1 = ((bf16[16,8,96,128]{3,2,1,0:T(8,128)(2,1)}), bf16[16,8,96,128]{3,2,1,0:T(8,128)(2,1)S(1)}, u32[]{:S(2)}, u32[]{:S(2)}) async-start(bf16[16,8,96,128]{3,2,1,0:T(8,128)(2,1)} %bitcast.8), calls=%async_computation.1 | async-start | bytes 6291456 | tf_op jit(solution)/shard_map/all_to_all | solution.py:232
  104.3 357.6 %all-reduce.2.cloned.1.call-start = ((), (), s32[]{:S(2)}) async-start(), calls=%async_computation.3 | async-start | bytes 6291456 | tf_op jit(solution)/shard_map/psum | solution.py:234
  144.0 2.7 copy-start
Sparse Core Ops, SparseCore 0:
  146.9 314.9 all-reduce.1

commit v2 on v1

v2 whole, which is shorter than its diff:
```python
import math

import jax
import jax.numpy as jnp
import numpy as np
from jax import lax
from jax.experimental import pallas as pl
from jax.experimental.pallas import tpu as pltpu
from jax.sharding import Mesh, PartitionSpec as P

FFT_LEN = 8192
TAPS = 16
LA = 128
HALF = LA // 2
REF = 32
OUTER = FFT_LEN // LA
SPECTRA = 96
HEAD = 64
TAIL = SPECTRA - HEAD
LEAD = 16
VMEM = 40 * 1024 * 1024


def make_tables():
    outer_row = np.arange(OUTER)
    angle_one = 2.0 * np.pi * np.outer(outer_row, outer_row) / OUTER
    first_table = np.concatenate([np.cos(angle_one), -np.sin(angle_one)], axis=1)
    inner_row = np.arange(LA)
    angle_twist = 2.0 * np.pi * np.outer(outer_row, inner_row) / FFT_LEN
    half_row = np.arange(HALF)
    angle_two = 2.0 * np.pi * np.outer(inner_row, half_row) / LA
    upper_rows = np.concatenate([np.cos(angle_two), -np.sin(angle_two)], axis=1)
    lower_rows = np.concatenate([np.sin(angle_two), np.cos(angle_two)], axis=1)
    second_table = np.concatenate([upper_rows, lower_rows], axis=0)
    second_table = second_table.reshape(2 * LA, 2, 2, 16, 2).transpose(0, 1, 3, 2, 4).reshape(2 * LA, 2, HALF)
    second_tables = np.stack([second_table.reshape(2 * LA, LA), second_table[:, ::-1].reshape(2 * LA, LA)])
    sample_pos = np.arange(TAPS * FFT_LEN)
    sinc_arg = np.pi * (sample_pos - TAPS * FFT_LEN / 2 + 0.5) / FFT_LEN
    proto = np.sin(sinc_arg) / sinc_arg
    proto = proto * (0.5 - 0.5 * np.cos(2.0 * np.pi * (sample_pos + 0.5) / (TAPS * FFT_LEN)))
    proto = proto / np.sqrt(np.mean(proto**2) * TAPS)
    taps = proto.reshape(TAPS, FFT_LEN)[::-1].reshape(TAPS, OUTER, LA)
    return (
        jnp.asarray(first_table.T, jnp.float32).astype(jnp.bfloat16),
        jnp.asarray(np.cos(angle_twist), jnp.float32),
        jnp.asarray(np.sin(angle_twist), jnp.float32),
        jnp.asarray(second_tables, jnp.float32).astype(jnp.bfloat16),
        jnp.asarray(taps, jnp.float32),
    )


def frames_kernel(x_ref, o0_ref, o1_ref, wide):
    for b in range(OUTER):
        wide[pl.ds(16 * b, 16), :] = x_ref[0, :, b * LA : (b + 1) * LA].astype(jnp.float32)
    for i in range(16):
        out = (o0_ref, o1_ref)[i % 2]
        for h in range(4):
            rows = wide[pl.ds(256 * h + i, 16, stride=16), :]
            out[i // 2, 0, h * 16 : (h + 1) * 16, :] = rows.astype(jnp.bfloat16)


def to_frames(by_time):
    times, inputs, _ = by_time.shape
    shape = jax.ShapeDtypeStruct((8, times, OUTER, LA), jnp.bfloat16)
    spec = pl.BlockSpec((8, 1, OUTER, LA), lambda s: (0, s, 0, 0))
    return pl.pallas_call(
        frames_kernel,
        grid=(times,),
        in_specs=[pl.BlockSpec((1, inputs, FFT_LEN), lambda s: (s, 0, 0))],
        out_specs=[spec, spec],
        out_shape=[shape, shape],
        scratch_shapes=[pltpu.VMEM((inputs * OUTER, LA), jnp.float32)],
        compiler_params=pltpu.CompilerParams(vmem_limit_bytes=VMEM),
        name="frames",
    )(by_time)


def filter_frames(x_ref, taps_ref, held, filt):
    held[0:LEAD] = jnp.zeros((LEAD, OUTER, LA), jnp.bfloat16)
    for t in range(8):
        held[LEAD + 12 * t : LEAD + 12 * t + 12] = x_ref[t]

    def step(n, carry):
        row = pl.multiple_of((n % 4) * 16, 16)
        base = (n // 4) * 8
        acc = [None] * 8
        for m in range(8 + TAPS - 1):
            v = held[base + (LEAD - TAPS + 1) + m, pl.ds(row, 16), :].astype(jnp.float32)
            for j in range(8):
                p = j + TAPS - 1 - m
                if 0 <= p < TAPS:
                    term = taps_ref[p, pl.ds(row, 16), :] * v
                    acc[j] = term if acc[j] is None else acc[j] + term
        for j in range(8):
            filt[(n // 4) * 2 + j // 4, pl.ds(row, 16), (j % 4) * LA : (j % 4 + 1) * LA] = acc[j].astype(jnp.bfloat16)
        return carry

    lax.fori_loop(0, 4 * SPECTRA // 8, step, 0)


def transform_frames(gain_ref, first_ref, cos_ref, sin_ref, second_ref, filt, spec):
    first = first_ref[...]

    def step(g, carry):
        part = jnp.dot(first, filt[g], preferred_element_type=jnp.float32)
        cos = cos_ref[...]
        sin = sin_ref[...]
        rows = []
        for f in range(4):
            u = part[:OUTER, f * LA : (f + 1) * LA]
            v = part[OUTER:, f * LA : (f + 1) * LA]
            rows.append(jnp.concatenate([u * cos + v * sin, v * cos - u * sin], axis=1).astype(jnp.bfloat16))
        for h in range(2):
            turned = jnp.concatenate([row[h * 32 : h * 32 + 32] for row in rows], axis=0)
            whole = jnp.dot(turned, second_ref[h], preferred_element_type=jnp.float32)
            gain = gain_ref[h * 32 : h * 32 + 32]
            for f in range(4):
                start = pl.multiple_of((g * 4 + f) * OUTER + h * 32, 32)
                spec[pl.ds(start, 32), :] = whole[f * 32 : f * 32 + 32] * gain
        return carry

    lax.fori_loop(0, SPECTRA // 4, step, 0)


def turn_spectra(t4, spec, head, tail, tail_row):
    low = lax.broadcasted_iota(jnp.int32, (LA, LA), 1) < HALF
    low_all = lax.broadcasted_iota(jnp.int32, (SPECTRA, LA), 1) < HALF
    low_half = lax.broadcasted_iota(jnp.int32, (HALF, LA), 1) < HALF
    for rp in range(4):
        tails = []
        for kp in range(2):
            k = t4 * 8 + rp * 2 + kp
            one = spec[pl.ds(k, SPECTRA, stride=OUTER), :]
            two = spec[pl.ds(k + 32, SPECTRA, stride=OUTER), :]
            re = jnp.where(low_all, one, two)
            im = jnp.where(low_all, two, one)
            whole = jnp.concatenate([re[:HEAD], im[:HEAD]], axis=0).T
            for k2 in range(2):
                start = (k2 * 8 + rp * 2 + kp) * HALF
                head[start : start + HALF, :] = jnp.where(
                    low_half, whole[k2 * HALF : k2 * HALF + HALF], whole[HALF - k2 * HALF : LA - k2 * HALF]
                )
            tails += [re[HEAD:], im[HEAD:]]
        whole = jnp.concatenate(tails, axis=0).T
        lane = lax.broadcasted_iota(jnp.int32, (HALF, LA), 1)
        real = (lane // TAIL) % 2 == 0
        for k2 in range(2):
            start = (k2 * 8 + tail_row + rp) * HALF
            tail[start : start + HALF, :] = jnp.where(
                real, whole[k2 * HALF : k2 * HALF + HALF], whole[HALF - k2 * HALF : LA - k2 * HALF]
            )


def spread(t4, groups, o_ref):
    for k2 in range(2):
        for q in range(HALF):
            rows = [group[pl.ds(k2 * 8 * HALF + q, 8, stride=HALF), :] for group in groups]
            o_ref[q // 4, (q % 4) * 8 + k2 * 4 + t4] = jnp.concatenate(rows, axis=0).astype(jnp.bfloat16)


def spectra_first_kernel(
    x_ref, gain_ref, first_ref, cos_ref, sin_ref, second_ref, taps_ref, head_ref, kept_ref, held, filt, spec, head, tail
):
    filter_frames(x_ref, taps_ref, held, filt)
    transform_frames(gain_ref, first_ref, cos_ref, sin_ref, second_ref, filt, spec)

    def step(t4, carry):
        turn_spectra(t4, spec, head, tail, 0)
        spread(t4, [head], head_ref)
        for k2 in range(2):
            kept_ref[t4, k2] = tail[k2 * 8 * HALF : (k2 * 8 + 4) * HALF, :].astype(jnp.bfloat16)
        return carry

    lax.fori_loop(0, 4, step, 0)


def spectra_second_kernel(
    x_ref, gain_ref, first_ref, cos_ref, sin_ref, second_ref, taps_ref, kept_ref, o_ref, held, filt, spec, head, tail
):
    filter_frames(x_ref, taps_ref, held, filt)
    transform_frames(gain_ref, first_ref, cos_ref, sin_ref, second_ref, filt, spec)

    def step(t4, carry):
        turn_spectra(t4, spec, head, tail, 4)
        for k2 in range(2):
            tail[k2 * 8 * HALF : (k2 * 8 + 4) * HALF, :] = kept_ref[t4, k2].astype(jnp.float32)
        spread(t4, [head, tail], o_ref)
        return carry

    lax.fori_loop(0, 4, step, 0)


def spectra(framed, gain, tables, kept=None):
    first = kept is None
    out = jax.ShapeDtypeStruct((16, 32, 8 if first else 16, LA), jnp.bfloat16)
    keep = jax.ShapeDtypeStruct((4, 2, 4 * HALF, LA), jnp.bfloat16)
    return pl.pallas_call(
        spectra_first_kernel if first else spectra_second_kernel,
        out_shape=[out, keep] if first else out,
        scratch_shapes=[
            pltpu.VMEM((LEAD + SPECTRA, OUTER, LA), jnp.bfloat16),
            pltpu.VMEM((SPECTRA // 4, OUTER, 4 * LA), jnp.bfloat16),
            pltpu.VMEM((SPECTRA * OUTER, LA), jnp.float32),
            pltpu.VMEM((16 * HALF, LA), jnp.float32),
            pltpu.VMEM((16 * HALF, LA), jnp.float32),
        ],
        compiler_params=pltpu.CompilerParams(vmem_limit_bytes=VMEM),
        cost_estimate=pl.CostEstimate(flops=2_000_000_000, bytes_accessed=4_000_000, transcendentals=0),
        name="spectra_first" if first else "spectra_second",
    )(framed, gain, *tables, *(() if first else (kept,)))


def cross_kernel(first_ref, second_ref, o_ref, head, tail):
    def place(z, carry):
        for s in range(32):
            at = (s // 16) * 256 + (s % 16) + z * 16
            head[pl.ds(pl.multiple_of(at * 16, 16), 8), :] = first_ref[z, s].astype(jnp.float32)
            head[pl.ds(pl.multiple_of(at * 16 + 8, 8), 8), :] = second_ref[z, s, 0:8].astype(jnp.float32)
            tail[pl.ds(pl.multiple_of(at * 8, 8), 8), :] = second_ref[z, s, 8:16].astype(jnp.float32)
        return carry

    lax.fori_loop(0, 16, place, 0)
    lane = lax.broadcasted_iota(jnp.int32, (REF, LA), 1)
    head_sign = jnp.where(lane < HALF, -1.0, 1.0)
    tail_real = (lane // TAIL) % 2 == 0
    tail_sign = jnp.where(tail_real, -1.0, 1.0)
    for r in range(8):
        mine = lane // HALF == r % 2
        ref_head = head[pl.ds(r, REF, stride=8), :]
        ref_tail = jnp.where(mine, tail[pl.ds(r // 2, REF, stride=4), :], 0.0)
        im_head = pltpu.roll(ref_head, HALF, 1) * head_sign
        im_tail = jnp.where(tail_real, pltpu.roll(ref_tail, LA - TAIL, 1), pltpu.roll(ref_tail, TAIL, 1)) * tail_sign
        weights = jnp.concatenate(
            [jnp.concatenate([ref_head, ref_tail], axis=1), jnp.concatenate([im_head, im_tail], axis=1)], axis=0
        ).astype(jnp.bfloat16)
        for c in range(4):
            rows = jnp.concatenate(
                [
                    head[pl.ds(c * 256 * 8 + r, 256, stride=8), :].astype(jnp.bfloat16),
                    tail[pl.ds(c * 256 * 4 + r // 2, 256, stride=4), :].astype(jnp.bfloat16),
                ],
                axis=1,
            )
            part = lax.dot_general(weights, rows, (((1,), (1,)), ((), ())), preferred_element_type=jnp.float32)
            part = part * (1.0 / SPECTRA)
            for n in range(2):
                o_ref[n, r, :, c * 256 : (c + 1) * 256] = part[n * REF : (n + 1) * REF]


def cross(first, second):
    return pl.pallas_call(
        cross_kernel,
        out_shape=jax.ShapeDtypeStruct((2, 8, REF, 1024), jnp.float32),
        scratch_shapes=[pltpu.VMEM((1024 * 8, LA), jnp.float32), pltpu.VMEM((512 * 8, LA), jnp.float32)],
        compiler_params=pltpu.CompilerParams(vmem_limit_bytes=VMEM),
        cost_estimate=pl.CostEstimate(flops=500_000_000, bytes_accessed=5_000_000, transcendentals=0),
        name="cross",
    )(first, second)


def share(spec):
    rows = spec.shape[2]
    flat = lax.all_to_all(spec.reshape(512, rows, LA), ("z", "yh", "core", "yl", "x"), 0, 0, tiled=True)
    return flat.reshape(16, 32, rows, LA)


def after(value, other):
    return lax.optimization_barrier((value, other))[0]


def shards(voltages, eq_gain):
    tables = make_tables()
    mine = lax.axis_index("yl") * 4 + lax.axis_index("x")
    gain = lax.dynamic_slice(eq_gain, (2 * mine, 0), (2, eq_gain.shape[1])) * (1.0 / math.sqrt(FFT_LEN))
    gain = gain.reshape(2, 2, 16, 2, OUTER).transpose(0, 4, 2, 1, 3).reshape(2, OUTER, HALF)
    gain = jnp.concatenate([gain, gain], axis=2)
    frames0, frames1 = to_frames(jnp.swapaxes(voltages, 0, 1))
    framed0 = lax.all_to_all(frames0, ("yl", "x"), 0, 0, tiled=True)
    framed1 = lax.all_to_all(after(frames1, framed0), ("yl", "x"), 0, 0, tiled=True)
    head0, kept = spectra(framed0, gain[0], tables)
    owned0 = share(after(head0, framed1))
    second = spectra(framed1, gain[1], tables, kept)
    return cross(owned0, share(after(second, owned0)))


def solution(mesh):
    fine = Mesh(mesh.devices.reshape(2, 16, 2, 2, 4), ("yh", "z", "core", "yl", "x"))
    chan, tm = ("yh", "z", "core"), ("yl", "x")
    return jax.shard_map(
        shards,
        mesh=fine,
        in_specs=(P(chan, tm, None), P(chan, None)),
        out_specs=P(None, chan + tm, None, None),
        check_vma=False,
    )
```

time: 553 us -> 256 us (0.46)
  the two profiles are of different devices: /device:TPU:34 before, /device:TPU:1 now
where the time goes in v2:
time: 256 us
  blocking collectives  134 us (52%)
  Pallas kernels  42.3 us (17%)
  waiting for transfers between devices  38.4 us (15%)
  starting transfers between devices  30.1 us (12%)
  local copies, waits for them, and re-layouts  9.58 us (4%)
    all_to_all x1, blocking collectives, share(): lax.all_to_all(spec.reshape(512, rows, LA), ('z', 'yh', 'core', 'yl', 'x'...  111 us
    all_to_all x1, waiting for transfers between devices, share(): lax.all_to_all(spec.reshape(512, rows, LA), ('z', 'yh', 'core', 'yl', 'x'...  37.3 us
    pallas_call x2, Pallas kernels, spectra(): pl.pallas_call(spectra_first_kernel if first else spectra_second_kernel,...  33.7 us
    all_to_all x1, starting transfers between devices, share(): lax.all_to_all(spec.reshape(512, rows, LA), ('z', 'yh', 'core', 'yl', 'x'...  26.4 us
    all_to_all x1, blocking collectives, shards(): framed0 = lax.all_to_all(frames0, ('yl', 'x'), 0, 0, tiled=True)  23.3 us
    unnamed x24, local copies, waits for them, and re-layouts  9.36 us
    pallas_call x1, Pallas kernels, to_frames(): pl.pallas_call(frames_kernel, grid=(times,), in_specs=[pl.BlockSpec((1, i...  5.27 us
  transfers between devices with their start and end apart: 2, of which 2 were waited for; matrix products, arithmetic and copies ran while one was open for 0% of the time, Pallas kernels for 13%

profile of v2, /device:TPU:1, one launch (start us, length us, event | category | flops | bytes accessed | tf_op | source)
XLA Modules:
  0.0 255.6 jit_solution(9910443375500232870)
XLA Ops:
  0.0 0.0 copy-start
  0.0 1.9 copy-done
  1.9 5.3 %frames.1 = (bf16[8,12,64,128]{3,2,1,0:T(8,128)(2,1)S(1)}, bf16[8,12,64,128]{3,2,1,0:T(8,128)(2,1)}) custom-call(bf16[12,16,8192]{2,1,0:T(8,128)(2,1)S(1)} %bitcast.14), custom_call_target="tpu_custom_call" | custom-call | tf_op jit(solution)/shard_map/frames/pallas_call | solution.py:66
  7.2 23.3 %all_to_all.20.x_ref = bf16[8,12,64,128]{3,2,1,0:T(8,128)(2,1)S(1)} all-to-all(bf16[8,12,64,128]{3,2,1,0:T(8,128)(2,1)S(1)} %get-tuple-element.12), channel_id=1, replica_groups=mesh['yh'=2,'z'=16,'core'=2,'yl'=2,'x'=4] {'yl','x'}, dimensions={0} | all-to-all | bytes 3145728 | tf_op jit(solution)/shard_map/all_to_all | solution.py:278
  30.5 0.0 copy-start.6
  30.5 0.0 copy-start.7
  30.5 3.7 %all-to-all-start.1 = ((bf16[8,12,64,128]{3,2,1,0:T(8,128)(2,1)}), bf16[8,12,64,128]{3,2,1,0:T(8,128)(2,1)S(1)}, u32[]{:S(2)}, u32[]{:S(2)}) async-start(bf16[8,12,64,128]{3,2,1,0:T(8,128)(2,1)} %get-tuple-element.15), calls=%async_computation.1 | async-start | bytes 3145728 | tf_op jit(solution)/shard_map/all_to_all | solution.py:279
  34.3 0.9 dynamic-slice_multiply_fusion
  35.2 0.1 reshape.18
  35.3 0.1 copy.10
  35.4 0.1 fusion.2
  35.5 0.0 copy-done.6
  35.5 0.0 copy-done.7
  35.5 0.0 copy-done.8
  35.5 0.0 copy-done.9
  35.6 0.0 copy-start.4
  35.6 1.0 copy-done.4
  36.6 16.0 %spectra_first.1 = (bf16[16,32,8,128]{3,2,1,0:T(8,128)(2,1)S(1)}, bf16[4,2,256,128]{3,2,1,0:T(8,128)(2,1)S(1)}) custom-call(bf16[8,12,64,128]{3,2,1,0:T(8,128)(2,1)S(1)} %all_to_all.20.x_ref, f32[64,128]{1,0:T(8,128)S(1)} %get-tuple-element.20.gain_ref, bf16[128,64]{1,0:T(8,128)(2,1)S(1)} %copy-done.7, f32[64,128]{1,0:T(8,128)S(1)} %copy-done.9, ...), custom_call_target="tpu_custom_call" | custom-call | flops 2000000000 | bytes 4000000 | tf_op jit(solution)/shard_map/spectra_first/pallas_call | solution.py:197
  52.6 0.0 copy-start.3
  52.6 1.0 copy-done.3
  53.6 0.8 copy-done.10
  54.4 1.1 all-to-all-done.1.x_ref
  55.5 1.1 copy-done.1
  56.7 26.4 %all-to-all-start.2 = ((bf16[512,8,128]{2,1,0:T(8,128)(2,1)}), bf16[512,8,128]{2,1,0:T(8,128)(2,1)S(1)}, u32[]{:S(2)}, u32[]{:S(2)}) async-start(bf16[512,8,128]{2,1,0:T(8,128)(2,1)} %bitcast.16), calls=%async_computation.2 | async-start | bytes 2097152 | tf_op jit(solution)/shard_map/all_to_all | solution.py:263
  83.1 0.0 copy-start.2
  83.1 1.4 copy-done.2
  84.5 1.0 copy-done.5
  85.5 1.0 copy-done.11
  86.6 17.7 %spectra_second.1 = bf16[16,32,16,128]{3,2,1,0:T(8,128)(2,1)S(1)} custom-call(bf16[8,12,64,128]{3,2,1,0:T(8,128)(2,1)S(1)} %copy-done.2, f32[64,128]{1,0:T(8,128)S(1)} %get-tuple-element.19.gain_ref, bf16[128,64]{1,0:T(8,128)(2,1)S(1)} %copy-done.7, f32[64,128]{1,0:T(8,128)S(1)} %copy-done.9, f32[64,128]{1,0:T(8,128)S(1)} %copy-done.8, ...), custom_call_target="tpu_custom_call" | custom-call | flops 2000000000 | bytes 4000000 | tf_op jit(solution)/shard_map/spectra_second/pallas_call | solution.py:197
  104.2 37.3 %all-to-all-done.2 = bf16[512,8,128]{2,1,0:T(8,128)(2,1)S(1)} async-done(((bf16[512,8,128]{2,1,0:T(8,128)(2,1)}), bf16[512,8,128]{2,1,0:T(8,128)(2,1)S(1)}, u32[]{:S(2)}, u32[]{:S(2)}) %all-to-all-start.2) | async-done | bytes 1048608 | tf_op jit(solution)/shard_map/all_to_all | solution.py:263
  141.5 110.8 %all_to_all.21 = bf16[512,16,128]{2,1,0:T(8,128)(2,1)S(1)} all-to-all(bf16[512,16,128]{2,1,0:T(8,128)(2,1)S(1)} %bitcast.15), channel_id=1, replica_groups=mesh['yh'=2,'z'=16,'core'=2,'yl'=2,'x'=4] {'z','yh','core','yl','x'}, dimensions={0} | all-to-all | bytes 4194304 | tf_op jit(solution)/shard_map/all_to_all | solution.py:263
  252.3 3.3 %cross.1 = f32[2,8,32,1024]{3,2,1,0:T(8,128)} custom-call(bf16[16,32,8,128]{3,2,1,0:T(8,128)(2,1)S(1)} %bitcast.13, bf16[16,32,16,128]{3,2,1,0:T(8,128)(2,1)S(1)} %bitcast.12), custom_call_target="tpu_custom_call" | custom-call | flops 500000000 | bytes 5000000 | tf_op jit(solution)/shard_map/cross/pallas_call | solution.py:251
  (7 shorter events, 0.0 us)
Async XLA Ops:
  0.0 1.9 copy-start
  30.5 5.0 %copy-start.6 = (bf16[2,256,128]{2,1,0:T(8,128)(2,1)S(1)}, bf16[2,256,128]{2,1,0:T(8,128)(2,1)}, u32[]{:S(2)}) copy-start(bf16[2,256,128]{2,1,0:T(8,128)(2,1)} %constant.37.second_ref) | copy-start | bytes 393220
  30.5 5.0 %copy-start.7 = (bf16[128,64]{1,0:T(8,128)(2,1)S(1)}, bf16[128,64]{1,0:T(8,128)(2,1)}, u32[]{:S(2)}) copy-start(bf16[128,64]{1,0:T(8,128)(2,1)} %constant.36.first_ref) | copy-start | bytes 49156
  30.5 5.0 %copy-start.8 = (f32[64,128]{1,0:T(8,128)S(1)}, f32[64,128]{1,0:T(8,128)}, u32[]{:S(2)}) copy-start(f32[64,128]{1,0:T(8,128)} %constant.31.clone.sin_ref) | copy-start | bytes 98308
  30.5 5.0 %copy-start.9 = (f32[64,128]{1,0:T(8,128)S(1)}, f32[64,128]{1,0:T(8,128)}, u32[]{:S(2)}) copy-start(f32[64,128]{1,0:T(8,128)} %constant.30.clone.cos_ref) | copy-start | bytes 98308
  30.5 25.0 %all-to-all-start.1 = ((bf16[8,12,64,128]{3,2,1,0:T(8,128)(2,1)}), bf16[8,12,64,128]{3,2,1,0:T(8,128)(2,1)S(1)}, u32[]{:S(2)}, u32[]{:S(2)}) async-start(bf16[8,12,64,128]{3,2,1,0:T(8,128)(2,1)} %get-tuple-element.15), calls=%async_computation.1 | async-start | bytes 3145728 | tf_op jit(solution)/shard_map/all_to_all | solution.py:279
  35.6 1.0 copy-start.4
  52.6 1.0 copy-start.3
  53.6 0.8 copy-start.10
  55.5 1.1 copy-start.1
  56.7 84.8 %all-to-all-start.2 = ((bf16[512,8,128]{2,1,0:T(8,128)(2,1)}), bf16[512,8,128]{2,1,0:T(8,128)(2,1)S(1)}, u32[]{:S(2)}, u32[]{:S(2)}) async-start(bf16[512,8,128]{2,1,0:T(8,128)(2,1)} %bitcast.16), calls=%async_computation.2 | async-start | bytes 2097152 | tf_op jit(solution)/shard_map/all_to_all | solution.py:263
  83.1 1.4 copy-start.2
  84.5 1.0 copy-start.5
  85.5 1.0 copy-start.11

commit v3 on v2

--- a/solution.py
+++ b/solution.py
@@ -18,6 +18,7 @@
 HEAD = 64
 TAIL = SPECTRA - HEAD
 LEAD = 16
+GROUP = 12
 VMEM = 40 * 1024 * 1024
 
 
@@ -50,26 +51,28 @@
 
 
 def frames_kernel(x_ref, o0_ref, o1_ref, wide):
-    for b in range(OUTER):
-        wide[pl.ds(16 * b, 16), :] = x_ref[0, :, b * LA : (b + 1) * LA].astype(jnp.float32)
-    for i in range(16):
-        out = (o0_ref, o1_ref)[i % 2]
-        for h in range(4):
-            rows = wide[pl.ds(256 * h + i, 16, stride=16), :]
-            out[i // 2, 0, h * 16 : (h + 1) * 16, :] = rows.astype(jnp.bfloat16)
+    for n in range(x_ref.shape[0]):
+        for b in range(OUTER):
+            wide[n, pl.ds(16 * b, 16), :] = x_ref[n, :, b * LA : (b + 1) * LA].astype(jnp.float32)
+        for i in range(16):
+            out = (o0_ref, o1_ref)[i % 2]
+            for h in range(4):
+                rows = wide[n, pl.ds(256 * h + i, 16, stride=16), :]
+                out[i // 2, n, h * 16 : (h + 1) * 16, :] = rows.astype(jnp.bfloat16)
 
 
 def to_frames(by_time):
     times, inputs, _ = by_time.shape
+    each = 3
     shape = jax.ShapeDtypeStruct((8, times, OUTER, LA), jnp.bfloat16)
-    spec = pl.BlockSpec((8, 1, OUTER, LA), lambda s: (0, s, 0, 0))
+    spec = pl.BlockSpec((8, each, OUTER, LA), lambda s: (0, s, 0, 0))
     return pl.pallas_call(
         frames_kernel,
-        grid=(times,),
-        in_specs=[pl.BlockSpec((1, inputs, FFT_LEN), lambda s: (s, 0, 0))],
+        grid=(times // each,),
+        in_specs=[pl.BlockSpec((each, inputs, FFT_LEN), lambda s: (s, 0, 0))],
         out_specs=[spec, spec],
         out_shape=[shape, shape],
-        scratch_shapes=[pltpu.VMEM((inputs * OUTER, LA), jnp.float32)],
+        scratch_shapes=[pltpu.VMEM((each, inputs * OUTER, LA), jnp.float32)],
         compiler_params=pltpu.CompilerParams(vmem_limit_bytes=VMEM),
         name="frames",
     )(by_time)
@@ -82,26 +85,28 @@
 
     def step(n, carry):
         row = pl.multiple_of((n % 4) * 16, 16)
-        base = (n // 4) * 8
-        acc = [None] * 8
-        for m in range(8 + TAPS - 1):
+        base = (n // 4) * GROUP
+        acc = [None] * GROUP
+        for m in range(GROUP + TAPS - 1):
             v = held[base + (LEAD - TAPS + 1) + m, pl.ds(row, 16), :].astype(jnp.float32)
-            for j in range(8):
+            for j in range(GROUP):
                 p = j + TAPS - 1 - m
                 if 0 <= p < TAPS:
                     term = taps_ref[p, pl.ds(row, 16), :] * v
                     acc[j] = term if acc[j] is None else acc[j] + term
-        for j in range(8):
-            filt[(n // 4) * 2 + j // 4, pl.ds(row, 16), (j % 4) * LA : (j % 4 + 1) * LA] = acc[j].astype(jnp.bfloat16)
-        return carry
-
-    lax.fori_loop(0, 4 * SPECTRA // 8, step, 0)
+        for j in range(GROUP):
+            filt[(n // 4) * (GROUP // 4) + j // 4, pl.ds(row, 16), (j % 4) * LA : (j % 4 + 1) * LA] = acc[j].astype(
+                jnp.bfloat16
+            )
+        return carry
+
+    lax.fori_loop(0, 4 * SPECTRA // GROUP, step, 0)
 
 
 def transform_frames(gain_ref, first_ref, cos_ref, sin_ref, second_ref, filt, spec):
     first = first_ref[...]
 
-    def step(g, carry):
+    def section_one(g):
         part = jnp.dot(first, filt[g], preferred_element_type=jnp.float32)
         cos = cos_ref[...]
         sin = sin_ref[...]
@@ -110,6 +115,9 @@
             u = part[:OUTER, f * LA : (f + 1) * LA]
             v = part[OUTER:, f * LA : (f + 1) * LA]
             rows.append(jnp.concatenate([u * cos + v * sin, v * cos - u * sin], axis=1).astype(jnp.bfloat16))
+        return rows
+
+    def section_two(g, rows):
         for h in range(2):
             turned = jnp.concatenate([row[h * 32 : h * 32 + 32] for row in rows], axis=0)
             whole = jnp.dot(turned, second_ref[h], preferred_element_type=jnp.float32)
@@ -117,9 +125,17 @@
             for f in range(4):
                 start = pl.multiple_of((g * 4 + f) * OUTER + h * 32, 32)
                 spec[pl.ds(start, 32), :] = whole[f * 32 : f * 32 + 32] * gain
-        return carry
-
-    lax.fori_loop(0, SPECTRA // 4, step, 0)
+
+    def step(n, carry):
+        earlier = section_one(4 * n)
+        for m in range(1, 4):
+            later = section_one(4 * n + m)
+            section_two(4 * n + m - 1, earlier)
+            earlier = later
+        section_two(4 * n + 3, earlier)
+        return carry
+
+    lax.fori_loop(0, SPECTRA // 16, step, 0)
 
 
 def turn_spectra(t4, spec, head, tail, tail_row):
@@ -151,11 +167,13 @@
             )
 
 
-def spread(t4, groups, o_ref):
+def spread(t4, groups, o_ref, base=0):
     for k2 in range(2):
         for q in range(HALF):
             rows = [group[pl.ds(k2 * 8 * HALF + q, 8, stride=HALF), :] for group in groups]
-            o_ref[q // 4, (q % 4) * 8 + k2 * 4 + t4] = jnp.concatenate(rows, axis=0).astype(jnp.bfloat16)
+            o_ref[q // 4, (q % 4) * 8 + k2 * 4 + t4, base : base + 8 * len(groups)] = jnp.concatenate(
+                rows, axis=0
+            ).astype(jnp.bfloat16)
 
 
 def spectra_first_kernel(
@@ -175,7 +193,7 @@
 
 
 def spectra_second_kernel(
-    x_ref, gain_ref, first_ref, cos_ref, sin_ref, second_ref, taps_ref, kept_ref, o_ref, held, filt, spec, head, tail
+    x_ref, gain_ref, first_ref, cos_ref, sin_ref, second_ref, taps_ref, other_ref, kept_ref, o_ref, held, filt, spec, head, tail
 ):
     filter_frames(x_ref, taps_ref, held, filt)
     transform_frames(gain_ref, first_ref, cos_ref, sin_ref, second_ref, filt, spec)
@@ -184,15 +202,18 @@
         turn_spectra(t4, spec, head, tail, 4)
         for k2 in range(2):
             tail[k2 * 8 * HALF : (k2 * 8 + 4) * HALF, :] = kept_ref[t4, k2].astype(jnp.float32)
-        spread(t4, [head, tail], o_ref)
+        spread(t4, [head, tail], o_ref, 8)
+        for n in range(4):
+            for d in range(32):
+                o_ref[4 * t4 + n, d, 0:8] = other_ref[4 * t4 + n, d]
         return carry
 
     lax.fori_loop(0, 4, step, 0)
 
 
-def spectra(framed, gain, tables, kept=None):
-    first = kept is None
-    out = jax.ShapeDtypeStruct((16, 32, 8 if first else 16, LA), jnp.bfloat16)
+def spectra(framed, gain, tables, *kept):
+    first = not kept
+    out = jax.ShapeDtypeStruct((16, 32, 8 if first else 24, LA), jnp.bfloat16)
     keep = jax.ShapeDtypeStruct((4, 2, 4 * HALF, LA), jnp.bfloat16)
     return pl.pallas_call(
         spectra_first_kernel if first else spectra_second_kernel,
@@ -207,16 +228,16 @@
         compiler_params=pltpu.CompilerParams(vmem_limit_bytes=VMEM),
         cost_estimate=pl.CostEstimate(flops=2_000_000_000, bytes_accessed=4_000_000, transcendentals=0),
         name="spectra_first" if first else "spectra_second",
-    )(framed, gain, *tables, *(() if first else (kept,)))
-
-
-def cross_kernel(first_ref, second_ref, o_ref, head, tail):
+    )(framed, gain, *tables, *kept)
+
+
+def cross_kernel(x_ref, o_ref, head, tail):
     def place(z, carry):
         for s in range(32):
             at = (s // 16) * 256 + (s % 16) + z * 16
-            head[pl.ds(pl.multiple_of(at * 16, 16), 8), :] = first_ref[z, s].astype(jnp.float32)
-            head[pl.ds(pl.multiple_of(at * 16 + 8, 8), 8), :] = second_ref[z, s, 0:8].astype(jnp.float32)
-            tail[pl.ds(pl.multiple_of(at * 8, 8), 8), :] = second_ref[z, s, 8:16].astype(jnp.float32)
+            head[pl.ds(pl.multiple_of(at * 16, 16), 8), :] = x_ref[z, s, 0:8].astype(jnp.float32)
+            head[pl.ds(pl.multiple_of(at * 16 + 8, 8), 8), :] = x_ref[z, s, 8:16].astype(jnp.float32)
+            tail[pl.ds(pl.multiple_of(at * 8, 8), 8), :] = x_ref[z, s, 16:24].astype(jnp.float32)
         return carry
 
     lax.fori_loop(0, 16, place, 0)
@@ -247,7 +268,7 @@
                 o_ref[n, r, :, c * 256 : (c + 1) * 256] = part[n * REF : (n + 1) * REF]
 
 
-def cross(first, second):
+def cross(owned):
     return pl.pallas_call(
         cross_kernel,
         out_shape=jax.ShapeDtypeStruct((2, 8, REF, 1024), jnp.float32),
@@ -255,7 +276,7 @@
         compiler_params=pltpu.CompilerParams(vmem_limit_bytes=VMEM),
         cost_estimate=pl.CostEstimate(flops=500_000_000, bytes_accessed=5_000_000, transcendentals=0),
         name="cross",
-    )(first, second)
+    )(owned)
 
 
 def share(spec):
@@ -278,9 +299,7 @@
     framed0 = lax.all_to_all(frames0, ("yl", "x"), 0, 0, tiled=True)
     framed1 = lax.all_to_all(after(frames1, framed0), ("yl", "x"), 0, 0, tiled=True)
     head0, kept = spectra(framed0, gain[0], tables)
-    owned0 = share(after(head0, framed1))
-    second = spectra(framed1, gain[1], tables, kept)
-    return cross(owned0, share(after(second, owned0)))
+    return cross(share(spectra(framed1, gain[1], tables, head0, kept)))
 
 
 def solution(mesh):

time: 256 us -> 244 us (0.953)
  blocking collectives: 134 us -> 194 us
  waiting for transfers between devices: 38.4 us -> 5.85 us
  starting transfers between devices: 30.1 us -> 3.73 us
  Pallas kernels: 42.3 us -> 31.1 us
    all_to_all x1, blocking collectives: 111 us -> 171 us  [share(): lax.all_to_all(spec.reshape(512, rows, LA), ('z', 'yh', 'core', 'yl', 'x'...]
    all_to_all x1 -> x0, waiting for transfers between devices: 37.3 us -> none  [share(): lax.all_to_all(spec.reshape(512, rows, LA), ('z', 'yh', 'core', 'yl', 'x'...]
    all_to_all x1 -> x0, starting transfers between devices: 26.4 us -> none  [share(): lax.all_to_all(spec.reshape(512, rows, LA), ('z', 'yh', 'core', 'yl', 'x'...]
    pallas_call x2, Pallas kernels: 33.7 us -> 24.5 us  [spectra(): pl.pallas_call(spectra_first_kernel if first else spectra_second_kernel,...]
    all_to_all x1, waiting for transfers between devices: 1.15 us -> 5.85 us  [shards(): lax.all_to_all(after(frames1, framed0), ('yl', 'x'), 0, 0, tiled=True)]
    unnamed x24 -> x22, local copies, waits for them, and re-layouts: 9.36 us -> 8.05 us
  transfers between devices with their start and end apart: 2 -> 1, of which waited for: 2 -> 1; matrix products, arithmetic and copies ran while one was open for 0% -> 1% of each run, Pallas kernels for 13% -> 5%
where the time goes in v3:
time: 244 us
  blocking collectives  194 us (80%)
  Pallas kernels  31.1 us (13%)
  local copies, waits for them, and re-layouts  8.27 us (3%)
  waiting for transfers between devices  5.85 us (2%)
  starting transfers between devices  3.73 us (2%)
    all_to_all x1, blocking collectives, share(): lax.all_to_all(spec.reshape(512, rows, LA), ('z', 'yh', 'core', 'yl', 'x'...  171 us
    pallas_call x2, Pallas kernels, spectra(): pl.pallas_call(spectra_first_kernel if first else spectra_second_kernel,...  24.5 us
    all_to_all x1, blocking collectives, shards(): framed0 = lax.all_to_all(frames0, ('yl', 'x'), 0, 0, tiled=True)  23.3 us
    unnamed x22, local copies, waits for them, and re-layouts  8.05 us
    all_to_all x1, waiting for transfers between devices, shards(): lax.all_to_all(after(frames1, framed0), ('yl', 'x'), 0, 0, tiled=True)  5.85 us
  transfers between devices with their start and end apart: 1, of which 1 were waited for; matrix products, arithmetic and copies ran while one was open for 1% of the time, Pallas kernels for 5%

profile of v3, /device:TPU:1, one launch (start us, length us, event | category | flops | bytes accessed | tf_op | source)
XLA Modules:
  0.0 243.9 jit_solution(12733690787584112299)
XLA Ops:
  0.0 0.0 copy-start
  0.0 1.9 copy-done
  1.9 3.2 %frames.1 = (bf16[8,12,64,128]{3,2,1,0:T(8,128)(2,1)S(1)}, bf16[8,12,64,128]{3,2,1,0:T(8,128)(2,1)}) custom-call(bf16[12,16,8192]{2,1,0:T(8,128)(2,1)S(1)} %bitcast.11), custom_call_target="tpu_custom_call" | custom-call | tf_op jit(solution)/shard_map/frames/pallas_call | solution.py:69
  5.1 23.3 %all_to_all.15.x_ref = bf16[8,12,64,128]{3,2,1,0:T(8,128)(2,1)S(1)} all-to-all(bf16[8,12,64,128]{3,2,1,0:T(8,128)(2,1)S(1)} %get-tuple-element.11), channel_id=1, replica_groups=mesh['yh'=2,'z'=16,'core'=2,'yl'=2,'x'=4] {'yl','x'}, dimensions={0} | all-to-all | bytes 3145728 | tf_op jit(solution)/shard_map/all_to_all | solution.py:299
  28.4 0.0 copy-start.3
  28.4 0.0 copy-start.4
  28.4 0.0 copy-start.5
  28.4 0.0 copy-start.6
  28.4 3.7 %all-to-all-start.1 = ((bf16[8,12,64,128]{3,2,1,0:T(8,128)(2,1)}), bf16[8,12,64,128]{3,2,1,0:T(8,128)(2,1)S(1)}, u32[]{:S(2)}, u32[]{:S(2)}) async-start(bf16[8,12,64,128]{3,2,1,0:T(8,128)(2,1)} %get-tuple-element.12), calls=%async_computation.1 | async-start | bytes 3145728 | tf_op jit(solution)/shard_map/all_to_all | solution.py:300
  32.2 0.9 dynamic-slice_multiply_fusion
  33.1 0.1 reshape.12
  33.3 0.1 copy.10
  33.3 0.1 fusion.2
  33.4 0.0 copy-done.3
  33.4 0.0 copy-done.4
  33.4 0.0 copy-done.5
  33.5 0.0 copy-done.6
  33.5 0.0 copy-start.1
  33.5 1.0 copy-done.1
  34.5 11.3 %spectra_first.1 = (bf16[16,32,8,128]{3,2,1,0:T(8,128)(2,1)S(1)}, bf16[4,2,256,128]{3,2,1,0:T(8,128)(2,1)S(1)}) custom-call(bf16[8,12,64,128]{3,2,1,0:T(8,128)(2,1)S(1)} %all_to_all.15.x_ref, f32[64,128]{1,0:T(8,128)S(1)} %get-tuple-element.15.gain_ref, bf16[128,64]{1,0:T(8,128)(2,1)S(1)} %copy-done.4, f32[64,128]{1,0:T(8,128)S(1)} %copy-done.6, ...), custom_call_target="tpu_custom_call" | custom-call | flops 2000000000 | bytes 4000000 | tf_op jit(solution)/shard_map/spectra_first/pallas_call | solution.py:218
  45.8 0.0 copy-start.7
  45.8 1.0 copy-done.7
  46.8 0.0 copy-start.9
  46.8 0.8 copy-done.9
  47.6 5.8 %all-to-all-done.1.x_ref = bf16[8,12,64,128]{3,2,1,0:T(8,128)(2,1)S(1)} async-done(((bf16[8,12,64,128]{3,2,1,0:T(8,128)(2,1)}), bf16[8,12,64,128]{3,2,1,0:T(8,128)(2,1)S(1)}, u32[]{:S(2)}, u32[]{:S(2)}) %all-to-all-start.1) | async-done | bytes 1572896 | tf_op jit(solution)/shard_map/all_to_all | solution.py:300
  53.5 0.0 copy-start.2
  53.5 1.0 copy-done.2
  54.5 1.2 copy-done.8
  55.7 1.0 copy-done.10
  56.8 13.3 %spectra_second.1 = bf16[16,32,24,128]{3,2,1,0:T(8,128)(2,1)S(1)} custom-call(bf16[8,12,64,128]{3,2,1,0:T(8,128)(2,1)S(1)} %all-to-all-done.1.x_ref, f32[64,128]{1,0:T(8,128)S(1)} %get-tuple-element.16.gain_ref, bf16[128,64]{1,0:T(8,128)(2,1)S(1)} %copy-done.4, f32[64,128]{1,0:T(8,128)S(1)} %copy-done.6, f32[64,128]{1,0:T(8,128)S(1)} %copy-done.5, ...), custom_call_target="tpu_custom_call" | custom-call | flops 2000000000 | bytes 4000000 | tf_op jit(solution)/shard_map/spectra_second/pallas_call | solution.py:218
  70.0 170.5 %all_to_all.16 = bf16[512,24,128]{2,1,0:T(8,128)(2,1)S(1)} all-to-all(bf16[512,24,128]{2,1,0:T(8,128)(2,1)S(1)} %bitcast.12), channel_id=1, replica_groups=mesh['yh'=2,'z'=16,'core'=2,'yl'=2,'x'=4] {'z','yh','core','yl','x'}, dimensions={0} | all-to-all | bytes 6291456 | tf_op jit(solution)/shard_map/all_to_all | solution.py:284
  240.6 3.3 %cross.1 = f32[2,8,32,1024]{3,2,1,0:T(8,128)} custom-call(bf16[16,32,24,128]{3,2,1,0:T(8,128)(2,1)S(1)} %bitcast.10), custom_call_target="tpu_custom_call" | custom-call | flops 500000000 | bytes 5000000 | tf_op jit(solution)/shard_map/cross/pallas_call | solution.py:272
  (3 shorter events, 0.0 us)
Async XLA Ops:
  0.0 1.9 copy-start
  28.4 5.0 %copy-start.3 = (bf16[2,256,128]{2,1,0:T(8,128)(2,1)S(1)}, bf16[2,256,128]{2,1,0:T(8,128)(2,1)}, u32[]{:S(2)}) copy-start(bf16[2,256,128]{2,1,0:T(8,128)(2,1)} %constant.37.second_ref) | copy-start | bytes 393220
  28.4 5.0 %copy-start.4 = (bf16[128,64]{1,0:T(8,128)(2,1)S(1)}, bf16[128,64]{1,0:T(8,128)(2,1)}, u32[]{:S(2)}) copy-start(bf16[128,64]{1,0:T(8,128)(2,1)} %constant.36.first_ref) | copy-start | bytes 49156
  28.4 5.0 %copy-start.5 = (f32[64,128]{1,0:T(8,128)S(1)}, f32[64,128]{1,0:T(8,128)}, u32[]{:S(2)}) copy-start(f32[64,128]{1,0:T(8,128)} %constant.31.clone.sin_ref) | copy-start | bytes 98308
  28.4 5.0 %copy-start.6 = (f32[64,128]{1,0:T(8,128)S(1)}, f32[64,128]{1,0:T(8,128)}, u32[]{:S(2)}) copy-start(f32[64,128]{1,0:T(8,128)} %constant.30.clone.cos_ref) | copy-start | bytes 98308
  28.4 25.0 %all-to-all-start.1 = ((bf16[8,12,64,128]{3,2,1,0:T(8,128)(2,1)}), bf16[8,12,64,128]{3,2,1,0:T(8,128)(2,1)S(1)}, u32[]{:S(2)}, u32[]{:S(2)}) async-start(bf16[8,12,64,128]{3,2,1,0:T(8,128)(2,1)} %get-tuple-element.12), calls=%async_computation.1 | async-start | bytes 3145728 | tf_op jit(solution)/shard_map/all_to_all | solution.py:300
  33.5 1.0 copy-start.1
  45.8 1.0 copy-start.7
  46.8 0.8 copy-start.9
  53.5 1.0 copy-start.2
  54.5 1.2 copy-start.8
  55.7 1.0 copy-start.10

commit v4 on v3

--- a/solution.py
+++ b/solution.py
@@ -19,6 +19,7 @@
 TAIL = SPECTRA - HEAD
 LEAD = 16
 GROUP = 12
+EARLY = 32
 VMEM = 40 * 1024 * 1024
 
 
@@ -55,52 +56,59 @@
         for b in range(OUTER):
             wide[n, pl.ds(16 * b, 16), :] = x_ref[n, :, b * LA : (b + 1) * LA].astype(jnp.float32)
         for i in range(16):
-            out = (o0_ref, o1_ref)[i % 2]
             for h in range(4):
-                rows = wide[n, pl.ds(256 * h + i, 16, stride=16), :]
-                out[i // 2, n, h * 16 : (h + 1) * 16, :] = rows.astype(jnp.bfloat16)
+                rows = wide[n, pl.ds(256 * h + i, 16, stride=16), :].astype(jnp.bfloat16)
+                at = (i % 2) * 4 + h
+                if at < 6:
+                    o0_ref[i // 2, n, at * 16 : at * 16 + 16, :] = rows
+                else:
+                    o1_ref[i // 2, n, at * 16 - 96 : at * 16 - 80, :] = rows
 
 
 def to_frames(by_time):
     times, inputs, _ = by_time.shape
     each = 3
-    shape = jax.ShapeDtypeStruct((8, times, OUTER, LA), jnp.bfloat16)
-    spec = pl.BlockSpec((8, each, OUTER, LA), lambda s: (0, s, 0, 0))
+    spec = lambda rows: pl.BlockSpec((8, each, rows, LA), lambda s: (0, s, 0, 0))
+    shape = lambda rows: jax.ShapeDtypeStruct((8, times, rows, LA), jnp.bfloat16)
     return pl.pallas_call(
         frames_kernel,
         grid=(times // each,),
         in_specs=[pl.BlockSpec((each, inputs, FFT_LEN), lambda s: (s, 0, 0))],
-        out_specs=[spec, spec],
-        out_shape=[shape, shape],
+        out_specs=[spec(OUTER + EARLY), spec(OUTER - EARLY)],
+        out_shape=[shape(OUTER + EARLY), shape(OUTER - EARLY)],
         scratch_shapes=[pltpu.VMEM((each, inputs * OUTER, LA), jnp.float32)],
-        compiler_params=pltpu.CompilerParams(vmem_limit_bytes=VMEM),
+        compiler_params=pltpu.CompilerParams(vmem_limit_bytes=62 * 1024 * 1024),
         name="frames",
     )(by_time)
 
 
-def filter_frames(x_ref, taps_ref, held, filt):
-    held[0:LEAD] = jnp.zeros((LEAD, OUTER, LA), jnp.bfloat16)
+def hold_frames(x_ref, held):
+    held[0:LEAD] = jnp.zeros((LEAD,) + held.shape[1:], jnp.bfloat16)
     for t in range(8):
         held[LEAD + 12 * t : LEAD + 12 * t + 12] = x_ref[t]
 
+
+def filter_frames(held, held_row, taps_ref, taps_row, filt, filt_row, rows):
+    strips = rows // 16
+
     def step(n, carry):
-        row = pl.multiple_of((n % 4) * 16, 16)
-        base = (n // 4) * GROUP
+        strip = pl.multiple_of((n % strips) * 16, 16)
+        group = n // strips
         acc = [None] * GROUP
         for m in range(GROUP + TAPS - 1):
-            v = held[base + (LEAD - TAPS + 1) + m, pl.ds(row, 16), :].astype(jnp.float32)
+            v = held[group * GROUP + (LEAD - TAPS + 1) + m, pl.ds(held_row + strip, 16), :].astype(jnp.float32)
             for j in range(GROUP):
                 p = j + TAPS - 1 - m
                 if 0 <= p < TAPS:
-                    term = taps_ref[p, pl.ds(row, 16), :] * v
+                    term = taps_ref[p, pl.ds(taps_row + strip, 16), :] * v
                     acc[j] = term if acc[j] is None else acc[j] + term
         for j in range(GROUP):
-            filt[(n // 4) * (GROUP // 4) + j // 4, pl.ds(row, 16), (j % 4) * LA : (j % 4 + 1) * LA] = acc[j].astype(
-                jnp.bfloat16
-            )
-        return carry
-
-    lax.fori_loop(0, 4 * SPECTRA // GROUP, step, 0)
+            filt[group * (GROUP // 4) + j // 4, pl.ds(filt_row + strip, 16), (j % 4) * LA : (j % 4 + 1) * LA] = acc[
+                j
+            ].astype(jnp.bfloat16)
+        return carry
+
+    lax.fori_loop(0, strips * SPECTRA // GROUP, step, 0)
 
 
 def transform_frames(gain_ref, first_ref, cos_ref, sin_ref, second_ref, filt, spec):
@@ -177,9 +185,12 @@
 
 
 def spectra_first_kernel(
-    x_ref, gain_ref, first_ref, cos_ref, sin_ref, second_ref, taps_ref, head_ref, kept_ref, held, filt, spec, head, tail
+    x_ref, gain_ref, first_ref, cos_ref, sin_ref, second_ref, taps_ref,
+    head_ref, kept_ref, early_ref, held, filt, spec, head, tail
 ):
-    filter_frames(x_ref, taps_ref, held, filt)
+    hold_frames(x_ref, held)
+    filter_frames(held, 0, taps_ref, 0, filt, 0, OUTER)
+    filter_frames(held, OUTER, taps_ref, 0, early_ref, 0, EARLY)
     transform_frames(gain_ref, first_ref, cos_ref, sin_ref, second_ref, filt, spec)
 
     def step(t4, carry):
@@ -193,42 +204,82 @@
 
 
 def spectra_second_kernel(
-    x_ref, gain_ref, first_ref, cos_ref, sin_ref, second_ref, taps_ref, other_ref, kept_ref, o_ref, held, filt, spec, head, tail
+    x_ref, gain_ref, first_ref, cos_ref, sin_ref, second_ref, taps_hbm, other_hbm, kept_hbm, early_hbm,
+    o_ref, held, filt, spec, head, tail, taps, other, kept, sems
 ):
-    filter_frames(x_ref, taps_ref, held, filt)
+    moves = [
+        pltpu.make_async_copy(taps_hbm, taps, sems.at[0]),
+        pltpu.make_async_copy(early_hbm, filt.at[:, pl.ds(0, EARLY), :], sems.at[1]),
+        pltpu.make_async_copy(other_hbm, other, sems.at[2]),
+        pltpu.make_async_copy(kept_hbm, kept, sems.at[3]),
+    ]
+    for move in moves:
+        move.start()
+    hold_frames(x_ref, held)
+    moves[0].wait()
+    filter_frames(held, 0, taps, EARLY, filt, EARLY, OUTER - EARLY)
+    for move in moves[1:]:
+        move.wait()
     transform_frames(gain_ref, first_ref, cos_ref, sin_ref, second_ref, filt, spec)
 
     def step(t4, carry):
         turn_spectra(t4, spec, head, tail, 4)
         for k2 in range(2):
-            tail[k2 * 8 * HALF : (k2 * 8 + 4) * HALF, :] = kept_ref[t4, k2].astype(jnp.float32)
+            tail[k2 * 8 * HALF : (k2 * 8 + 4) * HALF, :] = kept[t4, k2].astype(jnp.float32)
         spread(t4, [head, tail], o_ref, 8)
         for n in range(4):
             for d in range(32):
-                o_ref[4 * t4 + n, d, 0:8] = other_ref[4 * t4 + n, d]
+                o_ref[4 * t4 + n, d, 0:8] = other[4 * t4 + n, d]
         return carry
 
     lax.fori_loop(0, 4, step, 0)
 
 
-def spectra(framed, gain, tables, *kept):
-    first = not kept
-    out = jax.ShapeDtypeStruct((16, 32, 8 if first else 24, LA), jnp.bfloat16)
-    keep = jax.ShapeDtypeStruct((4, 2, 4 * HALF, LA), jnp.bfloat16)
+HEAD_SHAPE = (16, 32, 8, LA)
+KEPT_SHAPE = (4, 2, 4 * HALF, LA)
+EARLY_SHAPE = (SPECTRA // 4, EARLY, 4 * LA)
+
+
+def spectra_scratch(rows):
+    return [
+        pltpu.VMEM((LEAD + SPECTRA, rows, LA), jnp.bfloat16),
+        pltpu.VMEM((SPECTRA // 4, OUTER, 4 * LA), jnp.bfloat16),
+        pltpu.VMEM((SPECTRA * OUTER, LA), jnp.float32),
+        pltpu.VMEM((16 * HALF, LA), jnp.float32),
+        pltpu.VMEM((16 * HALF, LA), jnp.float32),
+    ]
+
+
+def spectra_first(framed, gain, tables):
     return pl.pallas_call(
-        spectra_first_kernel if first else spectra_second_kernel,
-        out_shape=[out, keep] if first else out,
-        scratch_shapes=[
-            pltpu.VMEM((LEAD + SPECTRA, OUTER, LA), jnp.bfloat16),
-            pltpu.VMEM((SPECTRA // 4, OUTER, 4 * LA), jnp.bfloat16),
-            pltpu.VMEM((SPECTRA * OUTER, LA), jnp.float32),
-            pltpu.VMEM((16 * HALF, LA), jnp.float32),
-            pltpu.VMEM((16 * HALF, LA), jnp.float32),
-        ],
+        spectra_first_kernel,
+        out_shape=[jax.ShapeDtypeStruct(shape, jnp.bfloat16) for shape in (HEAD_SHAPE, KEPT_SHAPE, EARLY_SHAPE)],
+        scratch_shapes=spectra_scratch(OUTER + EARLY),
         compiler_params=pltpu.CompilerParams(vmem_limit_bytes=VMEM),
         cost_estimate=pl.CostEstimate(flops=2_000_000_000, bytes_accessed=4_000_000, transcendentals=0),
-        name="spectra_first" if first else "spectra_second",
-    )(framed, gain, *tables, *kept)
+        name="spectra_first",
+    )(framed, gain, *tables)
+
+
+def spectra_second(framed, gain, tables, other, kept, early):
+    far = pl.BlockSpec(memory_space=pltpu.HBM)
+    near = pl.BlockSpec(memory_space=pltpu.VMEM)
+    return pl.pallas_call(
+        spectra_second_kernel,
+        in_specs=[near] * 6 + [far] * 4,
+        out_specs=near,
+        out_shape=jax.ShapeDtypeStruct((16, 32, 24, LA), jnp.bfloat16),
+        scratch_shapes=spectra_scratch(OUTER - EARLY)
+        + [
+            pltpu.VMEM((TAPS, OUTER, LA), jnp.float32),
+            pltpu.VMEM(HEAD_SHAPE, jnp.bfloat16),
+            pltpu.VMEM(KEPT_SHAPE, jnp.bfloat16),
+            pltpu.SemaphoreType.DMA((4,)),
+        ],
+        compiler_params=pltpu.CompilerParams(vmem_limit_bytes=54 * 1024 * 1024),
+        cost_estimate=pl.CostEstimate(flops=2_000_000_000, bytes_accessed=4_000_000, transcendentals=0),
+        name="spectra_second",
+    )(framed, gain, *tables, other, kept, early)
 
 
 def cross_kernel(x_ref, o_ref, head, tail):
@@ -298,8 +349,8 @@
     frames0, frames1 = to_frames(jnp.swapaxes(voltages, 0, 1))
     framed0 = lax.all_to_all(frames0, ("yl", "x"), 0, 0, tiled=True)
     framed1 = lax.all_to_all(after(frames1, framed0), ("yl", "x"), 0, 0, tiled=True)
-    head0, kept = spectra(framed0, gain[0], tables)
-    return cross(share(spectra(framed1, gain[1], tables, head0, kept)))
+    early = spectra_first(framed0, gain[0], tables)
+    return cross(share(spectra_second(framed1, gain[1], tables, *early)))
 
 
 def solution(mesh):

time: 244 us -> 256 us (1.049)
  waiting for transfers between devices: 5.85 us -> 29.8 us
  blocking collectives: 194 us -> 174 us
  starting transfers between devices: 3.73 us -> 10.2 us
  Pallas kernels: 31.1 us -> 36.9 us
  local copies, waits for them, and re-layouts: 8.27 us -> 2.89 us
    all_to_all x0 -> x1, waiting for transfers between devices: none -> 29.8 us  [shards(): framed0 = lax.all_to_all(frames0, ('yl', 'x'), 0, 0, tiled=True)]
    all_to_all x1 -> x0, blocking collectives: 23.3 us -> none  [shards(): framed0 = lax.all_to_all(frames0, ('yl', 'x'), 0, 0, tiled=True)]
    all_to_all x0 -> x1, starting transfers between devices: none -> 6.01 us  [shards(): framed0 = lax.all_to_all(frames0, ('yl', 'x'), 0, 0, tiled=True)]
    all_to_all x1, waiting for transfers between devices: 5.85 us -> 0.01 us  [shards(): lax.all_to_all(after(frames1, framed0), ('yl', 'x'), 0, 0, tiled=True)]
    unnamed x22 -> x16, local copies, waits for them, and re-layouts: 8.05 us -> 2.67 us
    pallas_call x2, Pallas kernels: 24.5 us -> 28.3 us  [the longest x1 15 us: spectra_second(): pl.pallas_call(spectra_second_kernel, in_specs=[near] * 6 + [far] * 4, ou...]
    all_to_all x1, blocking collectives: 171 us -> 174 us  [share(): lax.all_to_all(spec.reshape(512, rows, LA), ('z', 'yh', 'core', 'yl', 'x'...]
  transfers between devices with their start and end apart: 1 -> 2, of which waited for: 1 -> 1; matrix products, arithmetic and copies ran while one was open for 1% -> 1% of each run, Pallas kernels for 5% -> 5%
where the time goes in v4:
time: 256 us; the launch traced here: 255 us
  blocking collectives  174 us (68%)
  Pallas kernels  36.9 us (14%)
  waiting for transfers between devices  29.8 us (12%)
  starting transfers between devices  10.2 us (4%)
  local copies, waits for them, and re-layouts  2.89 us (1%)
    all_to_all x1, blocking collectives, share(): lax.all_to_all(spec.reshape(512, rows, LA), ('z', 'yh', 'core', 'yl', 'x'...  174 us
    all_to_all x1, waiting for transfers between devices, shards(): framed0 = lax.all_to_all(frames0, ('yl', 'x'), 0, 0, tiled=True)  29.8 us
    pallas_call x1, Pallas kernels, spectra_second(): pl.pallas_call(spectra_second_kernel, in_specs=[near] * 6 + [far] * 4, ou...  15 us
    pallas_call x1, Pallas kernels, spectra_first(): pl.pallas_call(spectra_first_kernel, out_shape=[jax.ShapeDtypeStruct(shap...  13.3 us
    all_to_all x1, starting transfers between devices, shards(): framed0 = lax.all_to_all(frames0, ('yl', 'x'), 0, 0, tiled=True)  6.01 us
    pallas_call x1, Pallas kernels, to_frames(): pl.pallas_call(frames_kernel, grid=(times // each,), in_specs=[pl.BlockSp...  5.33 us
  transfers between devices with their start and end apart: 2, of which 1 were waited for; matrix products, arithmetic and copies ran while one was open for 1% of the time, Pallas kernels for 5%

profile of v4, /device:TPU:1, one launch (start us, length us, event | category | flops | bytes accessed | tf_op | source)
XLA Modules:
  0.0 255.4 jit_solution(3839125809725290205)
XLA Ops:
  0.0 5.3 %frames.1 = (bf16[8,12,96,128]{3,2,1,0:T(8,128)(2,1)}, bf16[8,12,32,128]{3,2,1,0:T(8,128)(2,1)}) custom-call(bf16[12,16,8192]{2,1,0:T(8,128)(2,1)} %bitcast.11), custom_call_target="tpu_custom_call" | custom-call | tf_op jit(solution)/shard_map/frames/pallas_call | solution.py:73
  5.3 0.0 copy-start
  5.3 0.0 copy-start.1
  5.3 0.0 copy-start.2
  5.3 0.0 copy-start.3
  5.3 0.0 copy-start.4
  5.4 6.0 %all-to-all-start = ((bf16[8,12,96,128]{3,2,1,0:T(8,128)(2,1)}), bf16[8,12,96,128]{3,2,1,0:T(8,128)(2,1)S(1)}, u32[]{:S(2)}, u32[]{:S(2)}) async-start(bf16[8,12,96,128]{3,2,1,0:T(8,128)(2,1)} %get-tuple-element.12), calls=%async_computation | async-start | bytes 4718592 | tf_op jit(solution)/shard_map/all_to_all | solution.py:350
  11.4 29.8 %all-to-all-done.x_ref = bf16[8,12,96,128]{3,2,1,0:T(8,128)(2,1)S(1)} async-done(((bf16[8,12,96,128]{3,2,1,0:T(8,128)(2,1)}), bf16[8,12,96,128]{3,2,1,0:T(8,128)(2,1)S(1)}, u32[]{:S(2)}, u32[]{:S(2)}) %all-to-all-start) | async-done | bytes 2359328 | tf_op jit(solution)/shard_map/all_to_all | solution.py:350
  41.2 4.2 %all-to-all-start.1 = ((bf16[8,12,32,128]{3,2,1,0:T(8,128)(2,1)}), bf16[8,12,32,128]{3,2,1,0:T(8,128)(2,1)}, u32[]{:S(2)}, u32[]{:S(2)}) async-start(bf16[8,12,32,128]{3,2,1,0:T(8,128)(2,1)} %get-tuple-element.13), calls=%async_computation.1 | async-start | bytes 1572864 | tf_op jit(solution)/shard_map/all_to_all | solution.py:351
  45.4 0.9 dynamic-slice_multiply_fusion
  46.4 0.1 reshape.12
  46.5 0.1 copy.10
  46.6 0.7 fusion.2
  47.3 0.0 copy-done
  47.3 0.0 copy-done.1
  47.3 0.0 copy-done.2
  47.3 0.0 copy-done.3
  47.3 0.0 copy-done.4
  47.3 13.3 %spectra_first.1 = (bf16[16,32,8,128]{3,2,1,0:T(8,128)(2,1)S(1)}, bf16[4,2,256,128]{3,2,1,0:T(8,128)(2,1)S(1)}, bf16[24,32,512]{2,1,0:T(8,128)(2,1)S(1)}) custom-call(bf16[8,12,96,128]{3,2,1,0:T(8,128)(2,1)S(1)} %all-to-all-done.x_ref, f32[64,128]{1,0:T(8,128)S(1)} %get-tuple-element.17.gain_ref, bf16[128,64]{1,0:T(8,128)(2,1)S(1)} %copy-done.2, ...), custom_call_target="tpu_custom_call" | custom-call | flops 2000000000 | bytes 4000000 | tf_op jit(solution)/shard_map/spectra_first/pallas_call | solution.py:254
  60.6 0.0 copy-start.5
  60.6 1.0 copy-done.5
  61.6 0.0 copy-start.6
  61.6 0.9 copy-done.6
  62.5 0.0 copy-start.7
  62.5 0.8 copy-done.7
  63.3 0.0 all-to-all-done.1.x_ref
  63.3 15.0 %spectra_second.1 = bf16[16,32,24,128]{3,2,1,0:T(8,128)(2,1)} custom-call(bf16[8,12,32,128]{3,2,1,0:T(8,128)(2,1)} %all-to-all-done.1.x_ref, f32[64,128]{1,0:T(8,128)} %get-tuple-element.18.gain_ref, bf16[128,64]{1,0:T(8,128)(2,1)} %constant.36.first_ref, f32[64,128]{1,0:T(8,128)} %constant.30.clone.cos_ref, f32[64,128]{1,0:T(8,128)} %constant.31.clone.sin_ref, ...), custom_call_target="tpu_custom_call" | custom-call | flops 2000000000 | bytes 4000000 | tf_op jit(solution)/shard_map/spectra_second/pallas_call | solution.py:267
  78.3 173.8 %all_to_all.15 = bf16[512,24,128]{2,1,0:T(8,128)(2,1)S(1)} all-to-all(bf16[512,24,128]{2,1,0:T(8,128)(2,1)} %bitcast.12), channel_id=1, replica_groups=mesh['yh'=2,'z'=16,'core'=2,'yl'=2,'x'=4] {'z','yh','core','yl','x'}, dimensions={0} | all-to-all | bytes 6291456 | tf_op jit(solution)/shard_map/all_to_all | solution.py:335
  252.1 3.3 %cross.1 = f32[2,8,32,1024]{3,2,1,0:T(8,128)} custom-call(bf16[16,32,24,128]{3,2,1,0:T(8,128)(2,1)S(1)} %bitcast.10), custom_call_target="tpu_custom_call" | custom-call | flops 500000000 | bytes 5000000 | tf_op jit(solution)/shard_map/cross/pallas_call | solution.py:323
  (1 shorter events, 0.0 us)
Async XLA Ops:
  5.3 42.0 %copy-start = (f32[16,64,128]{2,1,0:T(8,128)S(1)}, f32[16,64,128]{2,1,0:T(8,128)}, u32[]{:S(2)}) copy-start(f32[16,64,128]{2,1,0:T(8,128)} %constant.33.clone.taps_ref.taps_hbm) | copy-start | bytes 1572868
  5.3 42.0 %copy-start.1 = (bf16[2,256,128]{2,1,0:T(8,128)(2,1)S(1)}, bf16[2,256,128]{2,1,0:T(8,128)(2,1)}, u32[]{:S(2)}) copy-start(bf16[2,256,128]{2,1,0:T(8,128)(2,1)} %constant.37.second_ref) | copy-start | bytes 393220
  5.3 42.0 %copy-start.2 = (bf16[128,64]{1,0:T(8,128)(2,1)S(1)}, bf16[128,64]{1,0:T(8,128)(2,1)}, u32[]{:S(2)}) copy-start(bf16[128,64]{1,0:T(8,128)(2,1)} %constant.36.first_ref) | copy-start | bytes 49156
  5.3 42.0 %copy-start.3 = (f32[64,128]{1,0:T(8,128)S(1)}, f32[64,128]{1,0:T(8,128)}, u32[]{:S(2)}) copy-start(f32[64,128]{1,0:T(8,128)} %constant.31.clone.sin_ref) | copy-start | bytes 98308
  5.3 42.0 %copy-start.4 = (f32[64,128]{1,0:T(8,128)S(1)}, f32[64,128]{1,0:T(8,128)}, u32[]{:S(2)}) copy-start(f32[64,128]{1,0:T(8,128)} %constant.30.clone.cos_ref) | copy-start | bytes 98308
  5.4 35.9 %all-to-all-start = ((bf16[8,12,96,128]{3,2,1,0:T(8,128)(2,1)}), bf16[8,12,96,128]{3,2,1,0:T(8,128)(2,1)S(1)}, u32[]{:S(2)}, u32[]{:S(2)}) async-start(bf16[8,12,96,128]{3,2,1,0:T(8,128)(2,1)} %get-tuple-element.12), calls=%async_computation | async-start | bytes 4718592 | tf_op jit(solution)/shard_map/all_to_all | solution.py:350
  41.2 22.1 %all-to-all-start.1 = ((bf16[8,12,32,128]{3,2,1,0:T(8,128)(2,1)}), bf16[8,12,32,128]{3,2,1,0:T(8,128)(2,1)}, u32[]{:S(2)}, u32[]{:S(2)}) async-start(bf16[8,12,32,128]{3,2,1,0:T(8,128)(2,1)} %get-tuple-element.13), calls=%async_computation.1 | async-start | bytes 1572864 | tf_op jit(solution)/shard_map/all_to_all | solution.py:351
  60.6 1.0 copy-start.5
  61.6 0.9 copy-start.6
  62.5 0.8 copy-start.7

commit v5 on v3

--- a/solution.py
+++ b/solution.py
@@ -19,6 +19,10 @@
 TAIL = SPECTRA - HEAD
 LEAD = 16
 GROUP = 12
+SPEC_PITCH = 72
+ROW_PITCH = 68
+WIDE_PITCH = 20
+CROSS_PITCH = 12
 VMEM = 40 * 1024 * 1024
 
 
@@ -53,11 +57,11 @@
 def frames_kernel(x_ref, o0_ref, o1_ref, wide):
     for n in range(x_ref.shape[0]):
         for b in range(OUTER):
-            wide[n, pl.ds(16 * b, 16), :] = x_ref[n, :, b * LA : (b + 1) * LA].astype(jnp.float32)
+            wide[n, pl.ds(WIDE_PITCH * b, 16), :] = x_ref[n, :, b * LA : (b + 1) * LA].astype(jnp.float32)
         for i in range(16):
             out = (o0_ref, o1_ref)[i % 2]
             for h in range(4):
-                rows = wide[n, pl.ds(256 * h + i, 16, stride=16), :]
+                rows = wide[n, pl.ds(16 * WIDE_PITCH * h + i, 16, stride=WIDE_PITCH), :]
                 out[i // 2, n, h * 16 : (h + 1) * 16, :] = rows.astype(jnp.bfloat16)
 
 
@@ -72,7 +76,7 @@
         in_specs=[pl.BlockSpec((each, inputs, FFT_LEN), lambda s: (s, 0, 0))],
         out_specs=[spec, spec],
         out_shape=[shape, shape],
-        scratch_shapes=[pltpu.VMEM((each, inputs * OUTER, LA), jnp.float32)],
+        scratch_shapes=[pltpu.VMEM((each, OUTER * WIDE_PITCH, LA), jnp.float32)],
         compiler_params=pltpu.CompilerParams(vmem_limit_bytes=VMEM),
         name="frames",
     )(by_time)
@@ -123,19 +127,19 @@
             whole = jnp.dot(turned, second_ref[h], preferred_element_type=jnp.float32)
             gain = gain_ref[h * 32 : h * 32 + 32]
             for f in range(4):
-                start = pl.multiple_of((g * 4 + f) * OUTER + h * 32, 32)
+                start = pl.multiple_of((g * 4 + f) * SPEC_PITCH + h * 32, 8)
                 spec[pl.ds(start, 32), :] = whole[f * 32 : f * 32 + 32] * gain
 
     def step(n, carry):
-        earlier = section_one(4 * n)
-        for m in range(1, 4):
-            later = section_one(4 * n + m)
-            section_two(4 * n + m - 1, earlier)
+        earlier = section_one(8 * n)
+        for m in range(1, 8):
+            later = section_one(8 * n + m)
+            section_two(8 * n + m - 1, earlier)
             earlier = later
-        section_two(4 * n + 3, earlier)
-        return carry
-
-    lax.fori_loop(0, SPECTRA // 16, step, 0)
+        section_two(8 * n + 7, earlier)
+        return carry
+
+    lax.fori_loop(0, SPECTRA // 32, step, 0)
 
 
 def turn_spectra(t4, spec, head, tail, tail_row):
@@ -146,13 +150,13 @@
         tails = []
         for kp in range(2):
             k = t4 * 8 + rp * 2 + kp
-            one = spec[pl.ds(k, SPECTRA, stride=OUTER), :]
-            two = spec[pl.ds(k + 32, SPECTRA, stride=OUTER), :]
+            one = spec[pl.ds(k, SPECTRA, stride=SPEC_PITCH), :]
+            two = spec[pl.ds(k + 32, SPECTRA, stride=SPEC_PITCH), :]
             re = jnp.where(low_all, one, two)
             im = jnp.where(low_all, two, one)
             whole = jnp.concatenate([re[:HEAD], im[:HEAD]], axis=0).T
             for k2 in range(2):
-                start = (k2 * 8 + rp * 2 + kp) * HALF
+                start = (k2 * 8 + rp * 2 + kp) * ROW_PITCH
                 head[start : start + HALF, :] = jnp.where(
                     low_half, whole[k2 * HALF : k2 * HALF + HALF], whole[HALF - k2 * HALF : LA - k2 * HALF]
                 )
@@ -161,7 +165,7 @@
         lane = lax.broadcasted_iota(jnp.int32, (HALF, LA), 1)
         real = (lane // TAIL) % 2 == 0
         for k2 in range(2):
-            start = (k2 * 8 + tail_row + rp) * HALF
+            start = (k2 * 8 + tail_row + rp) * ROW_PITCH
             tail[start : start + HALF, :] = jnp.where(
                 real, whole[k2 * HALF : k2 * HALF + HALF], whole[HALF - k2 * HALF : LA - k2 * HALF]
             )
@@ -170,7 +174,7 @@
 def spread(t4, groups, o_ref, base=0):
     for k2 in range(2):
         for q in range(HALF):
-            rows = [group[pl.ds(k2 * 8 * HALF + q, 8, stride=HALF), :] for group in groups]
+            rows = [group[pl.ds(k2 * 8 * ROW_PITCH + q, 8, stride=ROW_PITCH), :] for group in groups]
             o_ref[q // 4, (q % 4) * 8 + k2 * 4 + t4, base : base + 8 * len(groups)] = jnp.concatenate(
                 rows, axis=0
             ).astype(jnp.bfloat16)
@@ -186,7 +190,9 @@
         turn_spectra(t4, spec, head, tail, 0)
         spread(t4, [head], head_ref)
         for k2 in range(2):
-            kept_ref[t4, k2] = tail[k2 * 8 * HALF : (k2 * 8 + 4) * HALF, :].astype(jnp.bfloat16)
+            for rp in range(4):
+                start = (k2 * 8 + rp) * ROW_PITCH
+                kept_ref[t4, k2, rp * HALF : rp * HALF + HALF] = tail[start : start + HALF, :].astype(jnp.bfloat16)
         return carry
 
     lax.fori_loop(0, 4, step, 0)
@@ -201,7 +207,9 @@
     def step(t4, carry):
         turn_spectra(t4, spec, head, tail, 4)
         for k2 in range(2):
-            tail[k2 * 8 * HALF : (k2 * 8 + 4) * HALF, :] = kept_ref[t4, k2].astype(jnp.float32)
+            for rp in range(4):
+                start = (k2 * 8 + rp) * ROW_PITCH
+                tail[start : start + HALF, :] = kept_ref[t4, k2, rp * HALF : rp * HALF + HALF].astype(jnp.float32)
         spread(t4, [head, tail], o_ref, 8)
         for n in range(4):
             for d in range(32):
@@ -221,9 +229,9 @@
         scratch_shapes=[
             pltpu.VMEM((LEAD + SPECTRA, OUTER, LA), jnp.bfloat16),
             pltpu.VMEM((SPECTRA // 4, OUTER, 4 * LA), jnp.bfloat16),
-            pltpu.VMEM((SPECTRA * OUTER, LA), jnp.float32),
-            pltpu.VMEM((16 * HALF, LA), jnp.float32),
-            pltpu.VMEM((16 * HALF, LA), jnp.float32),
+            pltpu.VMEM((SPECTRA * SPEC_PITCH, LA), jnp.float32),
+            pltpu.VMEM((16 * ROW_PITCH, LA), jnp.float32),
+            pltpu.VMEM((16 * ROW_PITCH, LA), jnp.float32),
         ],
         compiler_params=pltpu.CompilerParams(vmem_limit_bytes=VMEM),
         cost_estimate=pl.CostEstimate(flops=2_000_000_000, bytes_accessed=4_000_000, transcendentals=0),
@@ -235,8 +243,8 @@
     def place(z, carry):
         for s in range(32):
             at = (s // 16) * 256 + (s % 16) + z * 16
-            head[pl.ds(pl.multiple_of(at * 16, 16), 8), :] = x_ref[z, s, 0:8].astype(jnp.float32)
-            head[pl.ds(pl.multiple_of(at * 16 + 8, 8), 8), :] = x_ref[z, s, 8:16].astype(jnp.float32)
+            head[pl.ds(pl.multiple_of(at * 2 * CROSS_PITCH, 8), 8), :] = x_ref[z, s, 0:8].astype(jnp.float32)
+            head[pl.ds(pl.multiple_of(at * 2 * CROSS_PITCH, 8) + CROSS_PITCH, 8), :] = x_ref[z, s, 8:16].astype(jnp.float32)
             tail[pl.ds(pl.multiple_of(at * 8, 8), 8), :] = x_ref[z, s, 16:24].astype(jnp.float32)
         return carry
 
@@ -247,7 +255,7 @@
     tail_sign = jnp.where(tail_real, -1.0, 1.0)
     for r in range(8):
         mine = lane // HALF == r % 2
-        ref_head = head[pl.ds(r, REF, stride=8), :]
+        ref_head = head[pl.ds(r, REF, stride=CROSS_PITCH), :]
         ref_tail = jnp.where(mine, tail[pl.ds(r // 2, REF, stride=4), :], 0.0)
         im_head = pltpu.roll(ref_head, HALF, 1) * head_sign
         im_tail = jnp.where(tail_real, pltpu.roll(ref_tail, LA - TAIL, 1), pltpu.roll(ref_tail, TAIL, 1)) * tail_sign
@@ -257,7 +265,7 @@
         for c in range(4):
             rows = jnp.concatenate(
                 [
-                    head[pl.ds(c * 256 * 8 + r, 256, stride=8), :].astype(jnp.bfloat16),
+                    head[pl.ds(c * 256 * CROSS_PITCH + r, 256, stride=CROSS_PITCH), :].astype(jnp.bfloat16),
                     tail[pl.ds(c * 256 * 4 + r // 2, 256, stride=4), :].astype(jnp.bfloat16),
                 ],
                 axis=1,
@@ -272,7 +280,7 @@
     return pl.pallas_call(
         cross_kernel,
         out_shape=jax.ShapeDtypeStruct((2, 8, REF, 1024), jnp.float32),
-        scratch_shapes=[pltpu.VMEM((1024 * 8, LA), jnp.float32), pltpu.VMEM((512 * 8, LA), jnp.float32)],
+        scratch_shapes=[pltpu.VMEM((1024 * CROSS_PITCH, LA), jnp.float32), pltpu.VMEM((512 * 8, LA), jnp.float32)],
         compiler_params=pltpu.CompilerParams(vmem_limit_bytes=VMEM),
         cost_estimate=pl.CostEstimate(flops=500_000_000, bytes_accessed=5_000_000, transcendentals=0),
         name="cross",

time: 244 us -> 239 us (0.980)
  Pallas kernels: 31.1 us -> 22.7 us
  waiting for transfers between devices: 5.85 us -> 8.65 us
    pallas_call x2, Pallas kernels: 24.5 us -> 17.4 us  [spectra(): pl.pallas_call(spectra_first_kernel if first else spectra_second_kernel,...]
    all_to_all x1, waiting for transfers between devices: 5.85 us -> 8.65 us  [shards(): lax.all_to_all(after(frames1, framed0), ('yl', 'x'), 0, 0, tiled=True)]
  transfers between devices with their start and end apart: 1 -> 1, of which waited for: 1 -> 1; matrix products, arithmetic and copies ran while one was open for 1% -> 1% of each run, Pallas kernels for 5% -> 4%
where the time goes in v5:
time: 239 us; the launch traced here: 238 us
  blocking collectives  194 us (81%)
  Pallas kernels  22.7 us (9%)
  waiting for transfers between devices  8.65 us (4%)
  local copies, waits for them, and re-layouts  8.27 us (3%)
  starting transfers between devices  3.73 us (2%)
    all_to_all x1, blocking collectives, share(): lax.all_to_all(spec.reshape(512, rows, LA), ('z', 'yh', 'core', 'yl', 'x'...  171 us
    all_to_all x1, blocking collectives, shards(): framed0 = lax.all_to_all(frames0, ('yl', 'x'), 0, 0, tiled=True)  23.3 us
    pallas_call x2, Pallas kernels, spectra(): pl.pallas_call(spectra_first_kernel if first else spectra_second_kernel,...  17.4 us
    all_to_all x1, waiting for transfers between devices, shards(): lax.all_to_all(after(frames1, framed0), ('yl', 'x'), 0, 0, tiled=True)  8.65 us
    unnamed x22, local copies, waits for them, and re-layouts  8.05 us
  transfers between devices with their start and end apart: 1, of which 1 were waited for; matrix products, arithmetic and copies ran while one was open for 1% of the time, Pallas kernels for 4%

profile of v5, /device:TPU:1, one launch (start us, length us, event | category | flops | bytes accessed | tf_op | source)
XLA Modules:
  0.0 238.4 jit_solution(7728078255523536572)
XLA Ops:
  0.0 0.0 copy-start
  0.0 1.9 copy-done
  1.9 2.2 frames.1
  4.1 23.3 %all_to_all.15.x_ref = bf16[8,12,64,128]{3,2,1,0:T(8,128)(2,1)S(1)} all-to-all(bf16[8,12,64,128]{3,2,1,0:T(8,128)(2,1)S(1)} %get-tuple-element.11), channel_id=1, replica_groups=mesh['yh'=2,'z'=16,'core'=2,'yl'=2,'x'=4] {'yl','x'}, dimensions={0} | all-to-all | bytes 3145728 | tf_op jit(solution)/shard_map/all_to_all | solution.py:307
  27.4 0.0 copy-start.3
  27.4 0.0 copy-start.4
  27.4 0.0 copy-start.5
  27.4 0.0 copy-start.6
  27.4 3.7 %all-to-all-start.1 = ((bf16[8,12,64,128]{3,2,1,0:T(8,128)(2,1)}), bf16[8,12,64,128]{3,2,1,0:T(8,128)(2,1)S(1)}, u32[]{:S(2)}, u32[]{:S(2)}) async-start(bf16[8,12,64,128]{3,2,1,0:T(8,128)(2,1)} %get-tuple-element.12), calls=%async_computation.1 | async-start | bytes 3145728 | tf_op jit(solution)/shard_map/all_to_all | solution.py:308
  31.1 0.9 dynamic-slice_multiply_fusion
  32.1 0.1 reshape.12
  32.2 0.1 copy.10
  32.3 0.1 fusion.2
  32.4 0.0 copy-done.3
  32.4 0.0 copy-done.4
  32.4 0.0 copy-done.5
  32.4 0.0 copy-done.6
  32.4 0.0 copy-start.1
  32.5 1.0 copy-done.1
  33.5 8.5 %spectra_first.1 = (bf16[16,32,8,128]{3,2,1,0:T(8,128)(2,1)S(1)}, bf16[4,2,256,128]{3,2,1,0:T(8,128)(2,1)S(1)}) custom-call(bf16[8,12,64,128]{3,2,1,0:T(8,128)(2,1)S(1)} %all_to_all.15.x_ref, f32[64,128]{1,0:T(8,128)S(1)} %get-tuple-element.15.gain_ref, bf16[128,64]{1,0:T(8,128)(2,1)S(1)} %copy-done.4, f32[64,128]{1,0:T(8,128)S(1)} %copy-done.6, ...), custom_call_target="tpu_custom_call" | custom-call | flops 2000000000 | bytes 4000000 | tf_op jit(solution)/shard_map/spectra_first/pallas_call | solution.py:226
  42.0 0.0 copy-start.7
  42.0 1.0 copy-done.7
  42.9 0.0 copy-start.9
  42.9 0.8 copy-done.9
  43.8 8.7 %all-to-all-done.1.x_ref = bf16[8,12,64,128]{3,2,1,0:T(8,128)(2,1)S(1)} async-done(((bf16[8,12,64,128]{3,2,1,0:T(8,128)(2,1)}), bf16[8,12,64,128]{3,2,1,0:T(8,128)(2,1)S(1)}, u32[]{:S(2)}, u32[]{:S(2)}) %all-to-all-start.1) | async-done | bytes 1572896 | tf_op jit(solution)/shard_map/all_to_all | solution.py:308
  52.4 0.0 copy-start.2
  52.4 1.0 copy-done.2
  53.5 1.2 copy-done.8
  54.7 1.0 copy-done.10
  55.7 8.9 %spectra_second.1 = bf16[16,32,24,128]{3,2,1,0:T(8,128)(2,1)S(1)} custom-call(bf16[8,12,64,128]{3,2,1,0:T(8,128)(2,1)S(1)} %all-to-all-done.1.x_ref, f32[64,128]{1,0:T(8,128)S(1)} %get-tuple-element.16.gain_ref, bf16[128,64]{1,0:T(8,128)(2,1)S(1)} %copy-done.4, f32[64,128]{1,0:T(8,128)S(1)} %copy-done.6, f32[64,128]{1,0:T(8,128)S(1)} %copy-done.5, ...), custom_call_target="tpu_custom_call" | custom-call | flops 2000000000 | bytes 4000000 | tf_op jit(solution)/shard_map/spectra_second/pallas_call | solution.py:226
  64.7 170.5 %all_to_all.16 = bf16[512,24,128]{2,1,0:T(8,128)(2,1)S(1)} all-to-all(bf16[512,24,128]{2,1,0:T(8,128)(2,1)S(1)} %bitcast.12), channel_id=1, replica_groups=mesh['yh'=2,'z'=16,'core'=2,'yl'=2,'x'=4] {'z','yh','core','yl','x'}, dimensions={0} | all-to-all | bytes 6291456 | tf_op jit(solution)/shard_map/all_to_all | solution.py:292
  235.2 3.2 %cross.1 = f32[2,8,32,1024]{3,2,1,0:T(8,128)} custom-call(bf16[16,32,24,128]{3,2,1,0:T(8,128)(2,1)S(1)} %bitcast.10), custom_call_target="tpu_custom_call" | custom-call | flops 500000000 | bytes 5000000 | tf_op jit(solution)/shard_map/cross/pallas_call | solution.py:280
  (3 shorter events, 0.0 us)
Async XLA Ops:
  0.0 1.9 copy-start
  27.4 5.0 %copy-start.3 = (bf16[2,256,128]{2,1,0:T(8,128)(2,1)S(1)}, bf16[2,256,128]{2,1,0:T(8,128)(2,1)}, u32[]{:S(2)}) copy-start(bf16[2,256,128]{2,1,0:T(8,128)(2,1)} %constant.37.second_ref) | copy-start | bytes 393220
  27.4 5.0 %copy-start.4 = (bf16[128,64]{1,0:T(8,128)(2,1)S(1)}, bf16[128,64]{1,0:T(8,128)(2,1)}, u32[]{:S(2)}) copy-start(bf16[128,64]{1,0:T(8,128)(2,1)} %constant.36.first_ref) | copy-start | bytes 49156
  27.4 5.0 %copy-start.5 = (f32[64,128]{1,0:T(8,128)S(1)}, f32[64,128]{1,0:T(8,128)}, u32[]{:S(2)}) copy-start(f32[64,128]{1,0:T(8,128)} %constant.31.clone.sin_ref) | copy-start | bytes 98308
  27.4 5.0 %copy-start.6 = (f32[64,128]{1,0:T(8,128)S(1)}, f32[64,128]{1,0:T(8,128)}, u32[]{:S(2)}) copy-start(f32[64,128]{1,0:T(8,128)} %constant.30.clone.cos_ref) | copy-start | bytes 98308
  27.4 25.0 %all-to-all-start.1 = ((bf16[8,12,64,128]{3,2,1,0:T(8,128)(2,1)}), bf16[8,12,64,128]{3,2,1,0:T(8,128)(2,1)S(1)}, u32[]{:S(2)}, u32[]{:S(2)}) async-start(bf16[8,12,64,128]{3,2,1,0:T(8,128)(2,1)} %get-tuple-element.12), calls=%async_computation.1 | async-start | bytes 3145728 | tf_op jit(solution)/shard_map/all_to_all | solution.py:308
  32.4 1.0 copy-start.1
  42.0 1.0 copy-start.7
  42.9 0.8 copy-start.9
  52.4 1.0 copy-start.2
  53.5 1.2 copy-start.8
  54.7 1.0 copy-start.10

commit v6 on v5

--- a/solution.py
+++ b/solution.py
@@ -54,38 +54,35 @@
     )
 
 
-def frames_kernel(x_ref, o0_ref, o1_ref, wide):
+def frames_kernel(x_ref, o_ref, wide):
     for n in range(x_ref.shape[0]):
         for b in range(OUTER):
             wide[n, pl.ds(WIDE_PITCH * b, 16), :] = x_ref[n, :, b * LA : (b + 1) * LA].astype(jnp.float32)
         for i in range(16):
-            out = (o0_ref, o1_ref)[i % 2]
             for h in range(4):
                 rows = wide[n, pl.ds(16 * WIDE_PITCH * h + i, 16, stride=WIDE_PITCH), :]
-                out[i // 2, n, h * 16 : (h + 1) * 16, :] = rows.astype(jnp.bfloat16)
+                o_ref[i // 2, i % 2, n, h * 16 : (h + 1) * 16, :] = rows.astype(jnp.bfloat16)
 
 
 def to_frames(by_time):
     times, inputs, _ = by_time.shape
-    each = 3
-    shape = jax.ShapeDtypeStruct((8, times, OUTER, LA), jnp.bfloat16)
-    spec = pl.BlockSpec((8, each, OUTER, LA), lambda s: (0, s, 0, 0))
+    each = 2
     return pl.pallas_call(
         frames_kernel,
         grid=(times // each,),
         in_specs=[pl.BlockSpec((each, inputs, FFT_LEN), lambda s: (s, 0, 0))],
-        out_specs=[spec, spec],
-        out_shape=[shape, shape],
+        out_specs=pl.BlockSpec((8, 2, each, OUTER, LA), lambda s: (0, 0, s, 0, 0)),
+        out_shape=jax.ShapeDtypeStruct((8, 2, times, OUTER, LA), jnp.bfloat16),
         scratch_shapes=[pltpu.VMEM((each, OUTER * WIDE_PITCH, LA), jnp.float32)],
-        compiler_params=pltpu.CompilerParams(vmem_limit_bytes=VMEM),
+        compiler_params=pltpu.CompilerParams(vmem_limit_bytes=62 * 1024 * 1024),
         name="frames",
     )(by_time)
 
 
-def filter_frames(x_ref, taps_ref, held, filt):
+def filter_frames(x_ref, i, taps_ref, held, filt):
     held[0:LEAD] = jnp.zeros((LEAD, OUTER, LA), jnp.bfloat16)
     for t in range(8):
-        held[LEAD + 12 * t : LEAD + 12 * t + 12] = x_ref[t]
+        held[LEAD + 12 * t : LEAD + 12 * t + 12] = x_ref[t, i]
 
     def step(n, carry):
         row = pl.multiple_of((n % 4) * 16, 16)
@@ -107,7 +104,7 @@
     lax.fori_loop(0, 4 * SPECTRA // GROUP, step, 0)
 
 
-def transform_frames(gain_ref, first_ref, cos_ref, sin_ref, second_ref, filt, spec):
+def transform_frames(i, gain_ref, first_ref, cos_ref, sin_ref, second_ref, filt, spec):
     first = first_ref[...]
 
     def section_one(g):
@@ -125,10 +122,10 @@
         for h in range(2):
             turned = jnp.concatenate([row[h * 32 : h * 32 + 32] for row in rows], axis=0)
             whole = jnp.dot(turned, second_ref[h], preferred_element_type=jnp.float32)
-            gain = gain_ref[h * 32 : h * 32 + 32]
+            gain = gain_ref[i, h * 32 : h * 32 + 32]
             for f in range(4):
                 start = pl.multiple_of((g * 4 + f) * SPEC_PITCH + h * 32, 8)
-                spec[pl.ds(start, 32), :] = whole[f * 32 : f * 32 + 32] * gain
+                spec[i, pl.ds(start, 32), :] = whole[f * 32 : f * 32 + 32] * gain
 
     def step(n, carry):
         earlier = section_one(8 * n)
@@ -142,7 +139,7 @@
     lax.fori_loop(0, SPECTRA // 32, step, 0)
 
 
-def turn_spectra(t4, spec, head, tail, tail_row):
+def turn_spectra(t4, i, spec, head, tail):
     low = lax.broadcasted_iota(jnp.int32, (LA, LA), 1) < HALF
     low_all = lax.broadcasted_iota(jnp.int32, (SPECTRA, LA), 1) < HALF
     low_half = lax.broadcasted_iota(jnp.int32, (HALF, LA), 1) < HALF
@@ -150,14 +147,14 @@
         tails = []
         for kp in range(2):
             k = t4 * 8 + rp * 2 + kp
-            one = spec[pl.ds(k, SPECTRA, stride=SPEC_PITCH), :]
-            two = spec[pl.ds(k + 32, SPECTRA, stride=SPEC_PITCH), :]
+            one = spec[i, pl.ds(k, SPECTRA, stride=SPEC_PITCH), :]
+            two = spec[i, pl.ds(k + 32, SPECTRA, stride=SPEC_PITCH), :]
             re = jnp.where(low_all, one, two)
             im = jnp.where(low_all, two, one)
             whole = jnp.concatenate([re[:HEAD], im[:HEAD]], axis=0).T
             for k2 in range(2):
                 start = (k2 * 8 + rp * 2 + kp) * ROW_PITCH
-                head[start : start + HALF, :] = jnp.where(
+                head[i, start : start + HALF, :] = jnp.where(
                     low_half, whole[k2 * HALF : k2 * HALF + HALF], whole[HALF - k2 * HALF : LA - k2 * HALF]
                 )
             tails += [re[HEAD:], im[HEAD:]]
@@ -165,78 +162,50 @@
         lane = lax.broadcasted_iota(jnp.int32, (HALF, LA), 1)
         real = (lane // TAIL) % 2 == 0
         for k2 in range(2):
-            start = (k2 * 8 + tail_row + rp) * ROW_PITCH
+            start = (k2 * 8 + i * 4 + rp) * ROW_PITCH
             tail[start : start + HALF, :] = jnp.where(
                 real, whole[k2 * HALF : k2 * HALF + HALF], whole[HALF - k2 * HALF : LA - k2 * HALF]
             )
 
 
-def spread(t4, groups, o_ref, base=0):
+def spread(t4, head, tail, o_ref):
     for k2 in range(2):
         for q in range(HALF):
-            rows = [group[pl.ds(k2 * 8 * ROW_PITCH + q, 8, stride=ROW_PITCH), :] for group in groups]
-            o_ref[q // 4, (q % 4) * 8 + k2 * 4 + t4, base : base + 8 * len(groups)] = jnp.concatenate(
-                rows, axis=0
-            ).astype(jnp.bfloat16)
-
-
-def spectra_first_kernel(
-    x_ref, gain_ref, first_ref, cos_ref, sin_ref, second_ref, taps_ref, head_ref, kept_ref, held, filt, spec, head, tail
+            at = pl.ds(k2 * 8 * ROW_PITCH + q, 8, stride=ROW_PITCH)
+            rows = jnp.concatenate([head[0, at, :], head[1, at, :], tail[at, :]], axis=0)
+            o_ref[q // 4, (q % 4) * 8 + k2 * 4 + t4] = rows.astype(jnp.bfloat16)
+
+
+def spectra_kernel(
+    x_ref, gain_ref, first_ref, cos_ref, sin_ref, second_ref, taps_ref, o_ref, held, filt, spec, head, tail
 ):
-    filter_frames(x_ref, taps_ref, held, filt)
-    transform_frames(gain_ref, first_ref, cos_ref, sin_ref, second_ref, filt, spec)
+    for i in range(2):
+        filter_frames(x_ref, i, taps_ref, held, filt)
+        transform_frames(i, gain_ref, first_ref, cos_ref, sin_ref, second_ref, filt, spec)
 
     def step(t4, carry):
-        turn_spectra(t4, spec, head, tail, 0)
-        spread(t4, [head], head_ref)
-        for k2 in range(2):
-            for rp in range(4):
-                start = (k2 * 8 + rp) * ROW_PITCH
-                kept_ref[t4, k2, rp * HALF : rp * HALF + HALF] = tail[start : start + HALF, :].astype(jnp.bfloat16)
+        for i in range(2):
+            turn_spectra(t4, i, spec, head, tail)
+        spread(t4, head, tail, o_ref)
         return carry
 
     lax.fori_loop(0, 4, step, 0)
 
 
-def spectra_second_kernel(
-    x_ref, gain_ref, first_ref, cos_ref, sin_ref, second_ref, taps_ref, other_ref, kept_ref, o_ref, held, filt, spec, head, tail
-):
-    filter_frames(x_ref, taps_ref, held, filt)
-    transform_frames(gain_ref, first_ref, cos_ref, sin_ref, second_ref, filt, spec)
-
-    def step(t4, carry):
-        turn_spectra(t4, spec, head, tail, 4)
-        for k2 in range(2):
-            for rp in range(4):
-                start = (k2 * 8 + rp) * ROW_PITCH
-                tail[start : start + HALF, :] = kept_ref[t4, k2, rp * HALF : rp * HALF + HALF].astype(jnp.float32)
-        spread(t4, [head, tail], o_ref, 8)
-        for n in range(4):
-            for d in range(32):
-                o_ref[4 * t4 + n, d, 0:8] = other_ref[4 * t4 + n, d]
-        return carry
-
-    lax.fori_loop(0, 4, step, 0)
-
-
-def spectra(framed, gain, tables, *kept):
-    first = not kept
-    out = jax.ShapeDtypeStruct((16, 32, 8 if first else 24, LA), jnp.bfloat16)
-    keep = jax.ShapeDtypeStruct((4, 2, 4 * HALF, LA), jnp.bfloat16)
+def spectra(framed, gain, tables):
     return pl.pallas_call(
-        spectra_first_kernel if first else spectra_second_kernel,
-        out_shape=[out, keep] if first else out,
+        spectra_kernel,
+        out_shape=jax.ShapeDtypeStruct((16, 32, 24, LA), jnp.bfloat16),
         scratch_shapes=[
             pltpu.VMEM((LEAD + SPECTRA, OUTER, LA), jnp.bfloat16),
             pltpu.VMEM((SPECTRA // 4, OUTER, 4 * LA), jnp.bfloat16),
-            pltpu.VMEM((SPECTRA * SPEC_PITCH, LA), jnp.float32),
-            pltpu.VMEM((16 * ROW_PITCH, LA), jnp.float32),
+            pltpu.VMEM((2, SPECTRA * SPEC_PITCH, LA), jnp.float32),
+            pltpu.VMEM((2, 16 * ROW_PITCH, LA), jnp.float32),
             pltpu.VMEM((16 * ROW_PITCH, LA), jnp.float32),
         ],
         compiler_params=pltpu.CompilerParams(vmem_limit_bytes=VMEM),
-        cost_estimate=pl.CostEstimate(flops=2_000_000_000, bytes_accessed=4_000_000, transcendentals=0),
-        name="spectra_first" if first else "spectra_second",
-    )(framed, gain, *tables, *kept)
+        name="spectra",
+    )(framed, gain, *tables)
 
 
 def cross_kernel(x_ref, o_ref, head, tail):
@@ -293,21 +262,15 @@
     return flat.reshape(16, 32, rows, LA)
 
 
-def after(value, other):
-    return lax.optimization_barrier((value, other))[0]
-
-
 def shards(voltages, eq_gain):
     tables = make_tables()
     mine = lax.axis_index("yl") * 4 + lax.axis_index("x")
     gain = lax.dynamic_slice(eq_gain, (2 * mine, 0), (2, eq_gain.shape[1])) * (1.0 / math.sqrt(FFT_LEN))
     gain = gain.reshape(2, 2, 16, 2, OUTER).transpose(0, 4, 2, 1, 3).reshape(2, OUTER, HALF)
     gain = jnp.concatenate([gain, gain], axis=2)
-    frames0, frames1 = to_frames(jnp.swapaxes(voltages, 0, 1))
-    framed0 = lax.all_to_all(frames0, ("yl", "x"), 0, 0, tiled=True)
-    framed1 = lax.all_to_all(after(frames1, framed0), ("yl", "x"), 0, 0, tiled=True)
-    head0, kept = spectra(framed0, gain[0], tables)
-    return cross(share(spectra(framed1, gain[1], tables, head0, kept)))
+    frames = to_frames(jnp.swapaxes(voltages, 0, 1))
+    framed = lax.all_to_all(frames, ("yl", "x"), 0, 0, tiled=True)
+    return cross(share(spectra(framed, gain, tables)))
 
 
 def solution(mesh):

time: 239 us -> 248 us (1.038)
  waiting for transfers between devices: 8.65 us -> 37 us
  blocking collectives: 194 us -> 177 us
  local copies, waits for them, and re-layouts: 8.27 us -> 1.27 us
  Pallas kernels: 22.7 us -> 25.4 us
    all_to_all x1, waiting for transfers between devices: 8.65 us -> 37 us  [shards(): framed = lax.all_to_all(frames, ('yl', 'x'), 0, 0, tiled=True)]
    all_to_all x1 -> x0, blocking collectives: 23.3 us -> none  [shards(): framed0 = lax.all_to_all(frames0, ('yl', 'x'), 0, 0, tiled=True)]
    unnamed x22 -> x10, local copies, waits for them, and re-layouts: 8.05 us -> 1.05 us
    all_to_all x1, blocking collectives: 171 us -> 177 us  [share(): lax.all_to_all(spec.reshape(512, rows, LA), ('z', 'yh', 'core', 'yl', 'x'...]
    pallas_call x1, Pallas kernels: 2.16 us -> 5.59 us  [to_frames(): pl.pallas_call(frames_kernel, grid=(times // each,), in_specs=[pl.BlockSp...]
    pallas_call x2 -> x1, Pallas kernels: 17.4 us -> 16.6 us  [spectra(): pl.pallas_call(spectra_kernel, out_shape=jax.ShapeDtypeStruct((16, 32, 24...]
  transfers between devices with their start and end apart: 1 -> 1, of which waited for: 1 -> 1; matrix products, arithmetic and copies ran while one was open for 1% -> 0% of each run, Pallas kernels for 4% -> 0%
where the time goes in v6:
time: 248 us; the launch traced here: 247 us
  blocking collectives  177 us (71%)
  waiting for transfers between devices  37 us (15%)
  Pallas kernels  25.4 us (10%)
  starting transfers between devices  6.01 us (2%)
    all_to_all x1, blocking collectives, share(): lax.all_to_all(spec.reshape(512, rows, LA), ('z', 'yh', 'core', 'yl', 'x'...  177 us
    all_to_all x1, waiting for transfers between devices, shards(): framed = lax.all_to_all(frames, ('yl', 'x'), 0, 0, tiled=True)  37 us
    pallas_call x1, Pallas kernels, spectra(): pl.pallas_call(spectra_kernel, out_shape=jax.ShapeDtypeStruct((16, 32, 24...  16.6 us
    all_to_all x1, starting transfers between devices, shards(): framed = lax.all_to_all(frames, ('yl', 'x'), 0, 0, tiled=True)  6.01 us
    pallas_call x1, Pallas kernels, to_frames(): pl.pallas_call(frames_kernel, grid=(times // each,), in_specs=[pl.BlockSp...  5.59 us
  transfers between devices with their start and end apart: 1, of which 1 were waited for; matrix products, arithmetic and copies ran while one was open for 0% of the time, Pallas kernels for 0%

profile of v6, /device:TPU:1, one launch (start us, length us, event | category | flops | bytes accessed | tf_op | source)
XLA Modules:
  0.0 247.4 jit_solution(3192391182253158447)
XLA Ops:
  0.0 5.6 %frames.1 = bf16[8,2,12,64,128]{4,3,2,1,0:T(8,128)(2,1)} custom-call(bf16[12,16,8192]{2,1,0:T(8,128)(2,1)} %bitcast.8), custom_call_target="tpu_custom_call" | custom-call | tf_op jit(solution)/shard_map/frames/pallas_call | solution.py:70
  5.6 0.0 copy-start.1
  5.6 0.0 copy-start.2
  5.6 0.0 copy-start.3
  5.6 0.0 copy-start.4
  5.6 6.0 %all-to-all-start = ((bf16[8,2,12,64,128]{4,3,2,1,0:T(8,128)(2,1)}), bf16[8,2,12,64,128]{4,3,2,1,0:T(8,128)(2,1)S(1)}, u32[]{:S(2)}, u32[]{:S(2)}) async-start(bf16[8,2,12,64,128]{4,3,2,1,0:T(8,128)(2,1)} %frames.1), calls=%async_computation | async-start | bytes 6291456 | tf_op jit(solution)/shard_map/all_to_all | solution.py:272
  11.6 0.9 dynamic-slice_multiply_fusion
  12.5 0.1 reshape.12
  12.7 0.1 copy.10
  12.8 0.1 pad_maximum_fusion.gain_ref
  12.9 37.0 %all-to-all-done.x_ref = bf16[8,2,12,64,128]{4,3,2,1,0:T(8,128)(2,1)S(1)} async-done(((bf16[8,2,12,64,128]{4,3,2,1,0:T(8,128)(2,1)}), bf16[8,2,12,64,128]{4,3,2,1,0:T(8,128)(2,1)S(1)}, u32[]{:S(2)}, u32[]{:S(2)}) %all-to-all-start) | async-done | bytes 3145760 | tf_op jit(solution)/shard_map/all_to_all | solution.py:272
  49.9 0.0 copy-done.1
  49.9 0.0 copy-done.2
  49.9 0.0 copy-done.3
  49.9 0.0 copy-done.4
  49.9 0.0 copy-start
  49.9 1.0 copy-done
  51.0 16.6 %spectra.1 = bf16[16,32,24,128]{3,2,1,0:T(8,128)(2,1)S(1)} custom-call(bf16[8,2,12,64,128]{4,3,2,1,0:T(8,128)(2,1)S(1)} %all-to-all-done.x_ref, f32[2,64,128]{2,1,0:T(8,128)S(1)} %pad_maximum_fusion.gain_ref, bf16[128,64]{1,0:T(8,128)(2,1)S(1)} %copy-done.2, f32[64,128]{1,0:T(8,128)S(1)} %copy-done.3, f32[64,128]{1,0:T(8,128)S(1)} %copy-done.4, ...), custom_call_target="tpu_custom_call" | custom-call | tf_op jit(solution)/shard_map/spectra/pallas_call | solution.py:196
  67.6 176.6 %all_to_all.10 = bf16[512,24,128]{2,1,0:T(8,128)(2,1)S(1)} all-to-all(bf16[512,24,128]{2,1,0:T(8,128)(2,1)S(1)} %bitcast.6), channel_id=1, replica_groups=mesh['yh'=2,'z'=16,'core'=2,'yl'=2,'x'=4] {'z','yh','core','yl','x'}, dimensions={0} | all-to-all | bytes 6291456 | tf_op jit(solution)/shard_map/all_to_all | solution.py:261
  244.2 3.2 %cross.1 = f32[2,8,32,1024]{3,2,1,0:T(8,128)} custom-call(bf16[16,32,24,128]{3,2,1,0:T(8,128)(2,1)S(1)} %bitcast.7), custom_call_target="tpu_custom_call" | custom-call | flops 500000000 | bytes 5000000 | tf_op jit(solution)/shard_map/cross/pallas_call | solution.py:249
  (1 shorter events, 0.0 us)
Async XLA Ops:
  5.6 44.3 %copy-start.1 = (bf16[2,256,128]{2,1,0:T(8,128)(2,1)S(1)}, bf16[2,256,128]{2,1,0:T(8,128)(2,1)}, u32[]{:S(2)}) copy-start(bf16[2,256,128]{2,1,0:T(8,128)(2,1)} %constant.37.second_ref) | copy-start | bytes 393220
  5.6 44.3 %copy-start.2 = (bf16[128,64]{1,0:T(8,128)(2,1)S(1)}, bf16[128,64]{1,0:T(8,128)(2,1)}, u32[]{:S(2)}) copy-start(bf16[128,64]{1,0:T(8,128)(2,1)} %constant.36.first_ref) | copy-start | bytes 49156
  5.6 44.3 %copy-start.3 = (f32[64,128]{1,0:T(8,128)S(1)}, f32[64,128]{1,0:T(8,128)}, u32[]{:S(2)}) copy-start(f32[64,128]{1,0:T(8,128)} %constant.30.clone.cos_ref) | copy-start | bytes 98308
  5.6 44.3 %copy-start.4 = (f32[64,128]{1,0:T(8,128)S(1)}, f32[64,128]{1,0:T(8,128)}, u32[]{:S(2)}) copy-start(f32[64,128]{1,0:T(8,128)} %constant.31.clone.sin_ref) | copy-start | bytes 98308
  5.6 44.3 %all-to-all-start = ((bf16[8,2,12,64,128]{4,3,2,1,0:T(8,128)(2,1)}), bf16[8,2,12,64,128]{4,3,2,1,0:T(8,128)(2,1)S(1)}, u32[]{:S(2)}, u32[]{:S(2)}) async-start(bf16[8,2,12,64,128]{4,3,2,1,0:T(8,128)(2,1)} %frames.1), calls=%async_computation | async-start | bytes 6291456 | tf_op jit(solution)/shard_map/all_to_all | solution.py:272
  49.9 1.0 copy-start
